TPU v7x, 32 devices: a whole 2x2x4 slice. The times are simulated.
32 devices in a mesh: dp: 8 (over y, x, core), tensor: 4 (over z).
Axes of the slice: x: 2, y: 2, z: 4, core: 2. Of those that a mesh axis runs over, the one named last changes fastest.
Arguments:
- inputs: bfloat16 [16384, 1024], P(('dp', 'tensor')), may hold values from -6 to 6
- qkv_weight: bfloat16 [1024, 3072], P('dp', 'tensor'), may hold values from -0.25 to 0.25
- dense_weight: bfloat16 [1024, 1024], P('dp', 'tensor'), may hold values from -3 to 3
- expand_weight: bfloat16 [1024, 4096], P('dp', 'tensor'), may hold values from -0.1875 to 0.1875
- shrink_weight: bfloat16 [1024, 4096], P('dp', 'tensor'), may hold values from -0.09375 to 0.09375
- norm_gains: bfloat16 [2, 1024], P(None, 'dp'), may hold values from 0.5 to 1.5
- norm_biases: bfloat16 [2, 1024], P(None, 'dp'), may hold values from -3 to 3
- cotangent: bfloat16 [16384, 1024], P(('dp', 'tensor')), may hold values from -6 to 6
- segments: int32 [16384], P('dp'), may hold values from 0 to 4, as said below
Outputs:
- layer_out: bfloat16 [16384, 1024], P(('dp', 'tensor'))
- input_grad: float32 [16384, 1024], P(('dp', 'tensor'))
- qkv_grad: float32 [1024, 3072], P('dp', 'tensor')
- dense_grad: float32 [1024, 1024], P('dp', 'tensor')
- expand_grad: float32 [1024, 4096], P('dp', 'tensor')
- shrink_grad: float32 [1024, 4096], P('dp', 'tensor')
- attention_norm_grad: float32 [2, 1024], P(None, 'dp')
- feedforward_norm_grad: float32 [2, 1024], P(None, 'dp')
Inputs may be any that keep to these rules, and one draw needn't show every extreme that they name: `segments`: document numbers within each sequence of 2048 tokens never fall; attention joins tokens of one document.
All inputs are finite; a program needn't handle non-finite values.
Results may differ from a plain program's by a relative error of at most 0.013.
The roundings to bfloat16 on the way count: a program that leaves them out, or rounds other values in their place, can miss the bound.
Values may be sent and summed in bfloat16 or wider, within the bound.
No kernel may reach another device: no remote copies, remote signals or barrier semaphores. Data moves between devices by JAX's collectives and lax.ppermute only.
A program may use at most 192 MiB of HBM per device.

v0:
```python
from functools import partial

import jax
import jax.numpy as jnp
from jax import lax
from jax.sharding import PartitionSpec as P

HD = 64
ROT = 16
L = 2048
QB = 512


EPSILON = 1e-05
MASKED = -1e30


def rotary_tables(segments):
    grouped = segments.reshape(-1, L)
    places = jnp.arange(L, dtype=jnp.int32)
    change = jnp.concatenate(
        [jnp.ones((grouped.shape[0], 1), jnp.bool_), grouped[:, 1:] != grouped[:, :-1]], axis=1
    )
    starts = lax.cummax(jnp.where(change, places[None, :], 0), axis=1)
    position = (places[None, :] - starts).reshape(-1).astype(jnp.float32)
    frequency = 10000.0 ** (-(jnp.arange(ROT // 2, dtype=jnp.float32) * 2.0 / ROT))
    angles = position[:, None] * frequency[None, :]
    angles = jnp.concatenate([angles, angles], axis=1)
    return (jnp.cos(angles), jnp.sin(angles))


def rotate(values, cosine, sine):
    half_rot = ROT // 2
    head_part = values[..., :ROT]
    turned = jnp.concatenate([-head_part[..., half_rot:], head_part[..., :half_rot]], axis=-1)
    return jnp.concatenate(
        [head_part * cosine[:, None, :] + turned * sine[:, None, :], values[..., ROT:]], axis=-1
    )


def rotate_back(grads, cosine, sine):
    half_rot = ROT // 2
    head_part = grads[..., :ROT]
    sined = head_part * sine[:, None, :]
    turned_back = jnp.concatenate([sined[..., half_rot:], -sined[..., :half_rot]], axis=-1)
    return jnp.concatenate(
        [head_part * cosine[:, None, :] + turned_back, grads[..., ROT:]], axis=-1
    )


def norm_stats(rows):
    average = jnp.mean(rows, axis=-1, keepdims=True)
    centered = rows - average
    inv_scale = lax.rsqrt(jnp.mean(centered * centered, axis=-1, keepdims=True) + EPSILON)
    return (centered * inv_scale, inv_scale)


def normed_pair(normalized, gain_values, bias_values):
    first_norm = (normalized * gain_values[0] + bias_values[0]).astype(jnp.bfloat16)
    second_norm = (normalized * gain_values[1] + bias_values[1]).astype(jnp.bfloat16)
    return (first_norm, second_norm)


def norm_back(normalized, inv_scale, first_grad, second_grad, gain_values):
    scaled = first_grad * gain_values[0] + second_grad * gain_values[1]
    centered_grad = scaled - jnp.mean(scaled, axis=-1, keepdims=True)
    return inv_scale * (
        centered_grad - normalized * jnp.mean(scaled * normalized, axis=-1, keepdims=True)
    )


def norm_param_grads(normalized, first_grad, second_grad):
    attention_part = jnp.stack(
        [jnp.sum(first_grad * normalized, axis=0), jnp.sum(first_grad, axis=0)]
    )
    feedforward_part = jnp.stack(
        [jnp.sum(second_grad * normalized, axis=0), jnp.sum(second_grad, axis=0)]
    )
    return (attention_part, feedforward_part)


def contract_rows(left, right):
    return lax.dot_general(
        left, right, (((0,), (0,)), ((), ())), preferred_element_type=jnp.float32
    )


def times_transposed(left, right):
    return lax.dot_general(
        left, right, (((1,), (1,)), ((), ())), preferred_element_type=jnp.float32
    )


def block_inputs(queries, key_rows, value_rows, seg_grid, flat_index):
    block_count = queries.shape[1] // QB
    seq_index = flat_index // block_count
    block_start = flat_index % block_count * QB
    seq_queries = lax.dynamic_index_in_dim(queries, seq_index, 0, False)
    seq_keys = lax.dynamic_index_in_dim(key_rows, seq_index, 0, False)
    seq_values = lax.dynamic_index_in_dim(value_rows, seq_index, 0, False)
    seq_segments = lax.dynamic_index_in_dim(seg_grid, seq_index, 0, False)
    query_block = lax.dynamic_slice_in_dim(seq_queries, block_start, QB, 0)
    segment_block = lax.dynamic_slice_in_dim(seq_segments, block_start, QB, 0)
    row_index = block_start + jnp.arange(QB, dtype=jnp.int32)
    columns = jnp.arange(seq_segments.shape[0], dtype=jnp.int32)
    allowed = (segment_block[:, None] == seq_segments[None, :]) & (
        columns[None, :] <= row_index[:, None]
    )
    scores = jnp.einsum("qhd,khd->hqk", query_block, seq_keys, preferred_element_type=jnp.float32)
    scores = jnp.where(allowed[None], scores, MASKED)
    return (scores, query_block, seq_keys, seq_values, seq_index, block_start)


def attend(queries, key_rows, value_rows, seg_grid):
    seq_count, length, heads_here, head_size = queries.shape

    def forward_block(flat_index):
        scores, query_block, seq_keys, seq_values, seq_index, block_start = block_inputs(
            queries, key_rows, value_rows, seg_grid, flat_index
        )
        row_max = jnp.max(scores, axis=-1, keepdims=True)
        exponent = jnp.exp(scores - row_max)
        row_total = jnp.sum(exponent, axis=-1, keepdims=True)
        probabilities = (exponent / row_total).astype(jnp.bfloat16)
        block_out = jnp.einsum(
            "hqk,khd->qhd", probabilities, seq_values, preferred_element_type=jnp.float32
        )
        return (block_out.astype(jnp.bfloat16), (row_max + jnp.log(row_total))[..., 0])

    outputs, log_totals = lax.map(
        forward_block, jnp.arange(seq_count * (length // QB), dtype=jnp.int32)
    )
    return (outputs.reshape(seq_count, length, heads_here, head_size), log_totals)


def attend_back(queries, key_rows, value_rows, seg_grid, out_grad, log_totals):
    seq_count, length, heads_here, head_size = queries.shape
    block_count = length // QB

    def backward_block(flat_index):
        scores, query_block, seq_keys, seq_values, seq_index, block_start = block_inputs(
            queries, key_rows, value_rows, seg_grid, flat_index
        )
        totals_block = lax.dynamic_index_in_dim(log_totals, flat_index, 0, False)
        probabilities = jnp.exp(scores - totals_block[:, :, None])
        low_probs = probabilities.astype(jnp.bfloat16)
        seq_grad = lax.dynamic_index_in_dim(out_grad, seq_index, 0, False)
        grad_block = lax.dynamic_slice_in_dim(seq_grad, block_start, QB, 0)
        value_part = jnp.einsum(
            "hqk,qhd->khd", low_probs, grad_block, preferred_element_type=jnp.float32
        )
        prob_grad = jnp.einsum(
            "qhd,khd->hqk", grad_block, seq_values, preferred_element_type=jnp.float32
        )
        weighted = jnp.sum(probabilities * prob_grad, axis=-1, keepdims=True)
        score_grad = (probabilities * (prob_grad - weighted)).astype(jnp.bfloat16)
        query_part = jnp.einsum(
            "hqk,khd->qhd", score_grad, seq_keys, preferred_element_type=jnp.float32
        )
        key_part = jnp.einsum(
            "hqk,qhd->khd", score_grad, query_block, preferred_element_type=jnp.float32
        )
        return (query_part, key_part, value_part)

    query_parts, key_parts, value_parts = lax.map(
        backward_block, jnp.arange(seq_count * block_count, dtype=jnp.int32)
    )
    query_grad = query_parts.reshape(seq_count, length, heads_here, head_size)
    key_grad = jnp.sum(
        key_parts.reshape(seq_count, block_count, length, heads_here, head_size), axis=1
    )
    value_grad = jnp.sum(
        value_parts.reshape(seq_count, block_count, length, heads_here, head_size), axis=1
    )
    return (query_grad, key_grad, value_grad)


def on_device(
    inputs,
    qkv_weight,
    dense_weight,
    expand_weight,
    shrink_weight,
    norm_gains,
    norm_biases,
    cotangent,
    segments,
):
    full_qkv, full_dense, full_expand, full_shrink, full_gains, full_biases = (
        lax.all_gather(qkv_weight, "dp", axis=0, tiled=True),
        lax.all_gather(dense_weight, "dp", axis=0, tiled=True),
        lax.all_gather(expand_weight, "dp", axis=0, tiled=True),
        lax.all_gather(shrink_weight, "dp", axis=0, tiled=True),
        lax.all_gather(norm_gains, "dp", axis=1, tiled=True),
        lax.all_gather(norm_biases, "dp", axis=1, tiled=True),
    )
    gain_values = full_gains.astype(jnp.float32)
    bias_values = full_biases.astype(jnp.float32)
    heads_here = full_qkv.shape[1] // (3 * HD)
    own_hat, own_scale = norm_stats(inputs.astype(jnp.float32))
    first_local, second_local = normed_pair(own_hat, gain_values, bias_values)
    first_norm, second_norm = (
        lax.all_gather(first_local, "tensor", axis=0, tiled=True),
        lax.all_gather(second_local, "tensor", axis=0, tiled=True),
    )
    row_count = first_norm.shape[0]
    seq_count = row_count // L
    cosine, sine = rotary_tables(segments)
    seg_grid = segments.reshape(seq_count, L)
    projected = jnp.dot(first_norm, full_qkv, preferred_element_type=jnp.float32).reshape(
        row_count, heads_here, 3, HD
    )
    queries = (
        (rotate(projected[:, :, 0], cosine, sine) * HD ** (-0.5))
        .astype(jnp.bfloat16)
        .reshape(seq_count, L, heads_here, HD)
    )
    key_rows = (
        rotate(projected[:, :, 1], cosine, sine)
        .astype(jnp.bfloat16)
        .reshape(seq_count, L, heads_here, HD)
    )
    value_rows = projected[:, :, 2].astype(jnp.bfloat16).reshape(seq_count, L, heads_here, HD)
    attended, log_totals = attend(queries, key_rows, value_rows, seg_grid)
    attended_flat = attended.reshape(row_count, heads_here * HD)
    hidden_pre = jnp.dot(second_norm, full_expand, preferred_element_type=jnp.float32)
    activated = jax.nn.gelu(hidden_pre, approximate=False).astype(jnp.bfloat16)
    branches = times_transposed(attended_flat, full_dense) + times_transposed(
        activated, full_shrink
    )
    summed = lax.psum_scatter(
        branches.astype(jnp.bfloat16), "tensor", scatter_dimension=0, tiled=True
    ).astype(jnp.float32)
    layer_out = (inputs.astype(jnp.float32) + summed).astype(jnp.bfloat16)
    grad_rows = lax.all_gather(cotangent, "tensor", axis=0, tiled=True)
    dense_part = contract_rows(grad_rows, attended_flat)
    shrink_part = contract_rows(grad_rows, activated)
    attended_grad = (
        jnp.dot(grad_rows, full_dense, preferred_element_type=jnp.float32)
        .astype(jnp.bfloat16)
        .reshape(seq_count, L, heads_here, HD)
    )
    activated_grad = jnp.dot(grad_rows, full_shrink, preferred_element_type=jnp.float32)
    gelu_value, gelu_pull = jax.vjp(partial(jax.nn.gelu, approximate=False), hidden_pre)
    hidden_grad = gelu_pull(activated_grad)[0].astype(jnp.bfloat16)
    expand_part = contract_rows(second_norm, hidden_grad)
    second_grad = times_transposed(hidden_grad, full_expand)
    query_grad, key_grad, value_grad = attend_back(
        queries, key_rows, value_rows, seg_grid, attended_grad, log_totals
    )
    query_grad = rotate_back(
        query_grad.reshape(row_count, heads_here, HD) * HD ** (-0.5), cosine, sine
    )
    key_grad = rotate_back(key_grad.reshape(row_count, heads_here, HD), cosine, sine)
    projected_grad = jnp.stack(
        [query_grad, key_grad, value_grad.reshape(row_count, heads_here, HD)], axis=2
    )
    projected_grad = projected_grad.reshape(row_count, heads_here * 3 * HD).astype(jnp.bfloat16)
    qkv_part = contract_rows(first_norm, projected_grad)
    first_grad = times_transposed(projected_grad, full_qkv)
    first_grad, second_grad = (
        lax.psum_scatter(
            first_grad.astype(jnp.bfloat16), "tensor", scatter_dimension=0, tiled=True
        ).astype(jnp.float32),
        lax.psum_scatter(
            second_grad.astype(jnp.bfloat16), "tensor", scatter_dimension=0, tiled=True
        ).astype(jnp.float32),
    )
    input_grad = cotangent.astype(jnp.float32) + norm_back(
        own_hat, own_scale, first_grad, second_grad, gain_values
    )
    attention_part, feedforward_part = norm_param_grads(own_hat, first_grad, second_grad)
    qkv_grad, dense_grad, expand_grad, shrink_grad, attention_owned, feedforward_owned = (
        lax.psum_scatter(qkv_part, "dp", scatter_dimension=0, tiled=True),
        lax.psum_scatter(dense_part, "dp", scatter_dimension=0, tiled=True),
        lax.psum_scatter(expand_part, "dp", scatter_dimension=0, tiled=True),
        lax.psum_scatter(shrink_part, "dp", scatter_dimension=0, tiled=True),
        lax.psum_scatter(attention_part, "dp", scatter_dimension=1, tiled=True),
        lax.psum_scatter(feedforward_part, "dp", scatter_dimension=1, tiled=True),
    )
    attention_norm_grad, feedforward_norm_grad = lax.psum(
        (attention_owned, feedforward_owned), "tensor"
    )
    return (
        layer_out,
        input_grad,
        qkv_grad,
        dense_grad,
        expand_grad,
        shrink_grad,
        attention_norm_grad,
        feedforward_norm_grad,
    )


def solution(mesh):
    return jax.shard_map(
        on_device,
        mesh=mesh,
        in_specs=(
            P(("dp", "tensor"), None),
            P("dp", "tensor"),
            P("dp", "tensor"),
            P("dp", "tensor"),
            P("dp", "tensor"),
            P(None, "dp"),
            P(None, "dp"),
            P(("dp", "tensor"), None),
            P("dp"),
        ),
        out_specs=(
            P(("dp", "tensor"), None),
            P(("dp", "tensor"), None),
            P("dp", "tensor"),
            P("dp", "tensor"),
            P("dp", "tensor"),
            P("dp", "tensor"),
            P(None, "dp"),
            P(None, "dp"),
        ),
        check_vma=False,
    )
```

profile of v0, /device:TPU:0, one launch (start us, length us, event | category | flops | bytes accessed | tf_op | source)
XLA Modules:
  0.0 996.9 jit_solution(2362911065756478010)
XLA Ops:
  7.9 10.3 %all_gather.27 = bf16[2,1024]{1,0:T(2,128)(2,1)S(1)} all-gather(bf16[2,128]{1,0:T(2,128)(2,1)} %param.18), channel_id=1, replica_groups=mesh['dp'=8,'tensor'=4] {'dp'}, dimensions={1}, use_global_device_ids=true | all-gather | bytes 4608 | tf_op jit(solution)/shard_map/all_gather | solution.py:194
  18.3 8.6 all_gather.28
  38.5 10.1 %all_gather.31 = bf16[1024,256]{1,0:T(8,128)(2,1)} all-gather(bf16[128,256]{1,0:T(8,128)(2,1)S(1)} %copy-done.21), channel_id=1, replica_groups=mesh['dp'=8,'tensor'=4] {'dp'}, dimensions={0}, use_global_device_ids=true | all-gather | bytes 589824 | tf_op jit(solution)/shard_map/all_gather | solution.py:191
  48.6 72.7 %all-gather.7.cloned.1.call-done = bf16[2048,1024]{1,0:T(8,128)(2,1)} async-done(((bf16[512,1024]{1,0:T(8,128)(2,1)}), bf16[2048,1024]{1,0:T(8,128)(2,1)}) %all-gather.7.cloned.1.call-update) | async-done | bytes 4194320 | tf_op jit(solution)/shard_map/all_gather | solution.py:203
  131.4 75.9 %while.30 = (s32[]{:T(128)}, bf16[4,512,4,64]{1,3,2,0:T(8,128)(2,1)S(1)}, f32[4,4,512]{2,1,0:T(4,128)}, s32[4]{0:T(128)S(1)}, s32[1,2048]{1,0:T(1,128)}, /*index...) while((s32[]{:T(128)}, ...), condition=%wide.region_7.8_spmd, body=%wide.region_4.7_spmd.sunk | while | flops 1114765824 | bytes 57232188 | solution.py:130
  212.4 241.6 %while.31 = (s32[]{:T(128)}, f32[4,512,4,64]{1,3,2,0:T(8,128)}, f32[4,2048,4,64]{1,3,2,0:T(8,128)}, f32[4,2048,4,64]{1,3,2,0:T(8,128)}, s32[4]{0:T(128)S(1)}, /*...) while((s32[]{:T(128)}, f32[4,512,4,64]{1,3,2,0:T(8,128)}, ...), condition=%wide.region_11.12_spmd, body=%wide.region_9.11_spmd.sunk | while | flops 2737830400 | bytes 227094544 | solution.py:165
  215.1 9.2 fusion.153
  229.8 15.7 %multiply_reduce_fusion.2 = (f32[4,512]{1,0:T(4,128)}, f32[4,512,2048]{2,1,0:T(8,128)}) fusion(f32[4,512,2048]{2,1,0:T(8,128)} %fusion.153, f32[4,512]{1,0:T(4,128)S(1)} %dynamic-slice_bitcast_fusion.2, pred[512,2048]{1,0:T(8,128)(4,1)} %fusion.154, bf16[1,2048,4,64]{1,3,2,0:T(8,128)(2,1)} %get-tuple-element.570, ...), kind=kOutput, calls=%fused_computation.21.clone.1 | convolution fusion | flops 553646080 | bytes 35930116 | tf_op jit(solution)/shard_map/while/body/eval_jaxpr/qhd,khd->hqk/dot_general | solution.py:152
  247.2 8.3 multiply_convert_fusion.3
  275.7 9.1 fusion.153
  290.3 15.6 %multiply_reduce_fusion.2 = (f32[4,512]{1,0:T(4,128)}, f32[4,512,2048]{2,1,0:T(8,128)}) fusion(f32[4,512,2048]{2,1,0:T(8,128)} %fusion.153, f32[4,512]{1,0:T(4,128)S(1)} %dynamic-slice_bitcast_fusion.2, pred[512,2048]{1,0:T(8,128)(4,1)} %fusion.154, bf16[1,2048,4,64]{1,3,2,0:T(8,128)(2,1)} %get-tuple-element.570, ...), kind=kOutput, calls=%fused_computation.21.clone.1 | convolution fusion | flops 553646080 | bytes 35930116 | tf_op jit(solution)/shard_map/while/body/eval_jaxpr/qhd,khd->hqk/dot_general | solution.py:152
  307.4 8.2 multiply_convert_fusion.3
  336.0 9.1 fusion.153
  350.6 15.5 %multiply_reduce_fusion.2 = (f32[4,512]{1,0:T(4,128)}, f32[4,512,2048]{2,1,0:T(8,128)}) fusion(f32[4,512,2048]{2,1,0:T(8,128)} %fusion.153, f32[4,512]{1,0:T(4,128)S(1)} %dynamic-slice_bitcast_fusion.2, pred[512,2048]{1,0:T(8,128)(4,1)} %fusion.154, bf16[1,2048,4,64]{1,3,2,0:T(8,128)(2,1)} %get-tuple-element.570, ...), kind=kOutput, calls=%fused_computation.21.clone.1 | convolution fusion | flops 553646080 | bytes 35930116 | tf_op jit(solution)/shard_map/while/body/eval_jaxpr/qhd,khd->hqk/dot_general | solution.py:152
  367.7 8.2 multiply_convert_fusion.3
  396.1 9.0 fusion.153
  410.7 15.5 %multiply_reduce_fusion.2 = (f32[4,512]{1,0:T(4,128)}, f32[4,512,2048]{2,1,0:T(8,128)}) fusion(f32[4,512,2048]{2,1,0:T(8,128)} %fusion.153, f32[4,512]{1,0:T(4,128)S(1)} %dynamic-slice_bitcast_fusion.2, pred[512,2048]{1,0:T(8,128)(4,1)} %fusion.154, bf16[1,2048,4,64]{1,3,2,0:T(8,128)(2,1)} %get-tuple-element.570, ...), kind=kOutput, calls=%fused_computation.21.clone.1 | convolution fusion | flops 553646080 | bytes 35930116 | tf_op jit(solution)/shard_map/while/body/eval_jaxpr/qhd,khd->hqk/dot_general | solution.py:152
  427.9 8.2 multiply_convert_fusion.3
  480.1 10.7 %fusion.93 = f32[2048,1024]{1,0:T(8,128)} fusion(bf16[2048,1024]{1,0:T(8,128)(2,1)} %all-gather.11.cloned.1.call-done, bf16[1024,1024]{1,0:T(8,128)(2,1)} %all-gather.13.cloned.1.call-done), kind=kOutput, calls=%fused_computation.170 | convolution fusion | flops 4294967296 | bytes 14680064 | tf_op jit(solution)/shard_map/dot_general | solution.py:226
  490.8 27.5 %add_convert_fusion = (bf16[2048,1024]{1,0:T(8,128)(2,1)S(1)}, f32[2048,1024]{1,0:T(8,128)}) fusion(f32[2048,1024]{1,0:T(8,128)} %fusion.93, bf16[2048,1024]{1,0:T(8,128)(2,1)} %all-gather.17.cloned.1.call-done, bf16[1024,1024]{1,0:T(8,128)(2,1)} %all-gather.15.cloned.1.call-done), kind=kOutput, calls=%fused_computation.59 | convolution fusion | flops 4445962240 | bytes 27262976 | tf_op jit(solution)/shard_map/dot_general | solution.py:243
  541.6 8.2 convolution_bitcast_fusion.2
  560.5 74.8 %reduce-scatter.18.cloned.1.call-done = bf16[512,1024]{1,0:T(8,128)(2,1)} async-done(((bf16[2048,1024]{1,0:T(8,128)(2,1)}), bf16[512,1024]{1,0:T(8,128)(2,1)}) %reduce-scatter.18.cloned.1.call-update) | async-done | bytes 1048592 | tf_op jit(solution)/shard_map/reduce_scatter | solution.py:265
  640.9 8.3 fusion.95
  649.3 10.2 %fusion.96 = f32[1024,1024]{1,0:T(8,128)} fusion(bf16[2048,1024]{1,0:T(8,128)(2,1)} %all-gather.11.cloned.1.call-done, bf16[2048,1024]{1,0:T(8,128)(2,1)} %copy-done.29), kind=kOutput, calls=%fused_computation.173 | convolution fusion | flops 4294967296 | bytes 12582912 | tf_op jit(solution)/shard_map/dot_general | solution.py:83
  659.5 16.1 %reduce-scatter.22.cloned.1.call-done = f32[128,256]{0,1:T(8,128)} async-done(((f32[1024,256]{0,1:T(8,128)}), f32[128,256]{0,1:T(8,128)}) %reduce-scatter.22.cloned.1.call-update) | async-done | bytes 131088 | tf_op jit(solution)/shard_map/reduce_scatter | solution.py:275
  677.3 52.9 %reduce-scatter.26.cloned.1.call-done = f32[128,1024]{0,1:T(8,128)} async-done(((f32[1024,1024]{0,1:T(8,128)}), f32[128,1024]{0,1:T(8,128)}) %reduce-scatter.26.cloned.1.call-update) | async-done | bytes 524304 | tf_op jit(solution)/shard_map/reduce_scatter | solution.py:277
  732.2 77.2 %reduce-scatter.14.cloned.1.call-done = bf16[512,1024]{1,0:T(8,128)(2,1)} async-done(((bf16[2048,1024]{1,0:T(8,128)(2,1)}), bf16[512,1024]{1,0:T(8,128)(2,1)}) %reduce-scatter.14.cloned.1.call-update) | async-done | bytes 1048592 | tf_op jit(solution)/shard_map/reduce_scatter | solution.py:231
  813.6 33.3 %reduce-scatter.30.cloned.1.call-done = f32[128,2]{1,0:T(8,128)} async-done(((f32[1024,2]{1,0:T(8,128)}), f32[128,2]{1,0:T(8,128)}) %reduce-scatter.30.cloned.1.call-update) | async-done | bytes 1040
  847.8 36.7 %reduce-scatter.28.cloned.1.call-done = f32[128,2]{1,0:T(8,128)} async-done(((f32[1024,2]{1,0:T(8,128)}), f32[128,2]{1,0:T(8,128)}) %reduce-scatter.28.cloned.1.call-update) | async-done | bytes 1040
  885.4 12.2 %all-reduce = (f32[2,128]{1,0:T(2,128)}, f32[2,128]{1,0:T(2,128)}) all-reduce(f32[2,128]{1,0:T(2,128)S(1)} %copy.39, f32[2,128]{1,0:T(2,128)S(1)} %copy.41), channel_id=1, replica_groups=mesh['dp'=8,'tensor'=4] {'tensor'}, use_global_device_ids=true, to_apply=%region_25.26 | all-reduce | flops 512 | bytes 4096 | tf_op jit(solution)/shard_map/psum | solution.py:281
  897.6 36.9 %reduce-scatter.20.cloned.1.call-done = f32[128,768]{1,0:T(8,128)} async-done(((f32[1024,768]{1,0:T(8,128)}), f32[128,768]{1,0:T(8,128)}) %reduce-scatter.20.cloned.1.call-update) | async-done | bytes 393232 | tf_op jit(solution)/shard_map/reduce_scatter | solution.py:274
  934.6 55.5 %reduce-scatter.24.cloned.1.call-done = f32[128,1024]{1,0:T(8,128)} async-done(((f32[1024,1024]{1,0:T(8,128)}), f32[128,1024]{1,0:T(8,128)}) %reduce-scatter.24.cloned.1.call-update) | async-done | bytes 524304 | tf_op jit(solution)/shard_map/reduce_scatter | solution.py:276
  (280 shorter events, 266.8 us)
Async XLA Ops:
  7.2 41.4 %all-gather.9.cloned.1.call-start = ((), (), s32[]{:S(2)}) async-start(), calls=%async_computation.10 | async-start | bytes 1769472 | tf_op jit(solution)/shard_map/all_gather | solution.py:190
  7.9 113.4 %all-gather.7.cloned.1.call-start = ((), (), s32[]{:S(2)}) async-start(), calls=%async_computation.9 | async-start | bytes 5242880 | tf_op jit(solution)/shard_map/all_gather | solution.py:203
  33.8 173.5 %all-gather.17.cloned.1.call-start = ((), (), s32[]{:S(2)}) async-start(), calls=%async_computation.15 | async-start | bytes 5242880 | tf_op jit(solution)/shard_map/all_gather | solution.py:235
  34.6 445.5 %all-gather.13.cloned.1.call-start = ((), (), s32[]{:S(2)}) async-start(), calls=%async_computation.12 | async-start | bytes 2359296 | tf_op jit(solution)/shard_map/all_gather | solution.py:192
  35.2 445.0 %all-gather.11.cloned.1.call-start = ((), (), s32[]{:S(2)}) async-start(), calls=%async_computation.11 | async-start | bytes 5242880 | tf_op jit(solution)/shard_map/all_gather | solution.py:204
  35.7 455.1 %all-gather.15.cloned.1.call-start = ((), (), s32[]{:S(2)}) async-start(), calls=%async_computation.13 | async-start | bytes 2359296 | tf_op jit(solution)/shard_map/all_gather | solution.py:193
  36.3 524.1 %reduce-scatter.16.cloned.1.call-start = ((), (), s32[]{:S(2)}) async-start(), calls=%async_computation.16 | async-start | bytes 5242880 | tf_op jit(solution)/shard_map/reduce_scatter | solution.py:262
  38.5 91.5 %copy-start.11 = (f32[2048,16]{0,1:T(8,128)}, f32[2048,16]{0,1:T(8,128)S(1)}, u32[]{:S(2)}) copy-start(f32[2048,16]{0,1:T(8,128)S(1)} %get-tuple-element.353) | copy-start | bytes 393220
  38.5 91.5 %copy-start.13 = (f32[2048,16]{0,1:T(8,128)}, f32[2048,16]{0,1:T(8,128)S(1)}, u32[]{:S(2)}) copy-start(f32[2048,16]{0,1:T(8,128)S(1)} %get-tuple-element.352) | copy-start | bytes 393220
  131.4 76.0 %copy-start.9 = (bf16[1024,256]{1,0:T(8,128)(2,1)S(1)}, bf16[1024,256]{1,0:T(8,128)(2,1)}, u32[]{:S(2)}) copy-start(bf16[1024,256]{1,0:T(8,128)(2,1)} %all_gather.31) | copy-start | bytes 1572868
  229.8 16.1 %slice-start.2 = ((s8[16777216]{0:T(1024)(128)(4,1)}), s8[4194304]{0:T(1024)(128)(4,1)S(1)}, s32[]{:S(2)}) async-start(s8[16777216]{0:T(1024)(128)(4,1)} %bitcast.204), calls=%async_computation.26 | async-start | bytes 8388608 | tf_op jit(solution)/shard_map/while
  229.8 17.3 %slice-start.3 = ((s8[16777216]{0:T(1024)(128)(4,1)}), s8[4194304]{0:T(1024)(128)(4,1)S(1)}, s32[]{:S(2)}) async-start(s8[16777216]{0:T(1024)(128)(4,1)} %bitcast.204), calls=%async_computation.27 | async-start | bytes 8388608 | tf_op jit(solution)/shard_map/while
  290.2 16.0 %slice-start.2 = ((s8[16777216]{0:T(1024)(128)(4,1)}), s8[4194304]{0:T(1024)(128)(4,1)S(1)}, s32[]{:S(2)}) async-start(s8[16777216]{0:T(1024)(128)(4,1)} %bitcast.204), calls=%async_computation.26 | async-start | bytes 8388608 | tf_op jit(solution)/shard_map/while
  290.3 17.2 %slice-start.3 = ((s8[16777216]{0:T(1024)(128)(4,1)}), s8[4194304]{0:T(1024)(128)(4,1)S(1)}, s32[]{:S(2)}) async-start(s8[16777216]{0:T(1024)(128)(4,1)} %bitcast.204), calls=%async_computation.27 | async-start | bytes 8388608 | tf_op jit(solution)/shard_map/while
  350.6 17.1 %slice-start.3 = ((s8[16777216]{0:T(1024)(128)(4,1)}), s8[4194304]{0:T(1024)(128)(4,1)S(1)}, s32[]{:S(2)}) async-start(s8[16777216]{0:T(1024)(128)(4,1)} %bitcast.204), calls=%async_computation.27 | async-start | bytes 8388608 | tf_op jit(solution)/shard_map/while
  410.7 17.1 %slice-start.3 = ((s8[16777216]{0:T(1024)(128)(4,1)}), s8[4194304]{0:T(1024)(128)(4,1)S(1)}, s32[]{:S(2)}) async-start(s8[16777216]{0:T(1024)(128)(4,1)} %bitcast.204), calls=%async_computation.27 | async-start | bytes 8388608 | tf_op jit(solution)/shard_map/while
  480.0 155.2 %reduce-scatter.18.cloned.1.call-start = ((), (), s32[]{:S(2)}) async-start(), calls=%async_computation.17 | async-start | bytes 5242880 | tf_op jit(solution)/shard_map/reduce_scatter | solution.py:265
  490.8 29.4 %copy-start.27 = (bf16[1024,1024]{1,0:T(8,128)(2,1)S(1)}, bf16[1024,1024]{1,0:T(8,128)(2,1)}, u32[]{:S(2)}) copy-start(bf16[1024,1024]{1,0:T(8,128)(2,1)} %all-gather.13.cloned.1.call-done) | copy-start | bytes 6291460
  526.5 149.1 %reduce-scatter.22.cloned.1.call-start = ((), (), s32[]{:S(2)}) async-start(), calls=%async_computation.19 | async-start | bytes 1179648 | tf_op jit(solution)/shard_map/reduce_scatter | solution.py:275
  531.3 198.8 %reduce-scatter.26.cloned.1.call-start = ((), (), s32[]{:S(2)}) async-start(), calls=%async_computation.21 | async-start | bytes 4718592 | tf_op jit(solution)/shard_map/reduce_scatter | solution.py:277
  549.9 259.5 %reduce-scatter.14.cloned.1.call-start = ((), (), s32[]{:S(2)}) async-start(), calls=%async_computation.14 | async-start | bytes 5242880 | tf_op jit(solution)/shard_map/reduce_scatter | solution.py:231
  560.3 74.9 %copy-start.2 = (bf16[512,1024]{1,0:T(8,128)(2,1)S(1)}, bf16[512,1024]{1,0:T(8,128)(2,1)}, u32[]{:S(2)}) copy-start(bf16[512,1024]{1,0:T(8,128)(2,1)} %param.13) | copy-start | bytes 3145732
  560.3 74.9 %copy-start.18 = (f32[1,1024]{1,0:T(1,128)S(1)}, f32[1,1024]{1,0:T(1,128)}, u32[]{:S(2)}) copy-start(f32[1,1024]{1,0:T(1,128)} %copy-done.17) | copy-start | bytes 12292
  560.3 74.9 %copy-start.20 = (f32[1,1024]{1,0:T(1,128)S(1)}, f32[1,1024]{1,0:T(1,128)}, u32[]{:S(2)}) copy-start(f32[1,1024]{1,0:T(1,128)} %copy-done.19) | copy-start | bytes 12292
  560.3 74.9 %copy-start.23 = (f32[512]{0:T(512)S(1)}, f32[512]{0:T(512)}, u32[]{:S(2)}) copy-start(f32[512]{0:T(512)} %copy-done.22) | copy-start | bytes 6148
  560.3 74.9 %copy-start.25 = (f32[512]{0:T(512)S(1)}, f32[512]{0:T(512)}, u32[]{:S(2)}) copy-start(f32[512]{0:T(512)} %copy-done.24) | copy-start | bytes 6148
  560.4 286.6 %reduce-scatter.30.cloned.1.call-start = ((), (), s32[]{:S(2)}) async-start(), calls=%async_computation.23 | async-start | bytes 589824
  639.5 245.0 %reduce-scatter.28.cloned.1.call-start = ((), (), s32[]{:S(2)}) async-start(), calls=%async_computation.22 | async-start | bytes 589824
  640.7 293.9 %reduce-scatter.20.cloned.1.call-start = ((), (), s32[]{:S(2)}) async-start(), calls=%async_computation.18 | async-start | bytes 3538944 | tf_op jit(solution)/shard_map/reduce_scatter | solution.py:274
  649.2 340.9 %reduce-scatter.24.cloned.1.call-start = ((), (), s32[]{:S(2)}) async-start(), calls=%async_computation.20 | async-start | bytes 4718592 | tf_op jit(solution)/shard_map/reduce_scatter | solution.py:276
  659.4 149.9 %copy-start.4 = (bf16[512,1024]{1,0:T(8,128)(2,1)S(1)}, bf16[512,1024]{1,0:T(8,128)(2,1)}, u32[]{:S(2)}) copy-start(bf16[512,1024]{1,0:T(8,128)(2,1)} %reduce-scatter.16.cloned.1.call-done) | copy-start | bytes 3145732
  659.4 149.9 %copy-start.5 = (bf16[512,1024]{1,0:T(8,128)(2,1)S(1)}, bf16[512,1024]{1,0:T(8,128)(2,1)}, u32[]{:S(2)}) copy-start(bf16[512,1024]{1,0:T(8,128)(2,1)} %reduce-scatter.18.cloned.1.call-done) | copy-start | bytes 3145732
  (35 other events, 259.5 us)
Sparse Core Ops, SparseCore 0:
  9.9 28.4 all-gather.8
  40.5 80.6 all-gather.6
  122.8 79.2 all-gather.16
  203.9 26.4 all-gather.12
  231.8 80.7 all-gather.10
  314.3 26.4 all-gather.14
  480.2 75.3 reduce-scatter.15
  558.0 77.2 reduce-scatter.17
  639.0 36.5 reduce-scatter.21
  678.8 51.2 reduce-scatter.25
  732.5 76.7 reduce-scatter.13
  812.3 34.6 reduce-scatter.29
  850.3 34.1 reduce-scatter.27
  888.3 46.2 reduce-scatter.19
  938.7 51.3 reduce-scatter.23
where the time goes:
time: 1010 us; the launch traced here: 997 us
  waiting for transfers between devices  459 us (45%)
  matrix products  307 us (30%)
  other arithmetic  110 us (11%)
  local copies, waits for them, and re-layouts  42.3 us (4%)
  blocking collectives  41.2 us (4%)
  loops' own time  21.5 us (2%)
  between operations  14.7 us (1%)
    reduce_scatter x1, waiting for transfers between devices, on_device(): lax.psum_scatter(branches.astype(jnp.bfloat16), 'tensor', scatter_dimensi...  77.2 us
    reduce_scatter x1, waiting for transfers between devices, on_device(): lax.psum_scatter(second_grad.astype(jnp.bfloat16), 'tensor', scatter_dime...  74.8 us
    unnamed x17, waiting for transfers between devices  73.1 us
    all_gather x1, waiting for transfers between devices, on_device(): lax.all_gather(first_local, 'tensor', axis=0, tiled=True)  72.7 us
    dot_general x4, matrix products, backward_block(): jnp.einsum('qhd,khd->hqk', grad_block, seq_values, preferred_element_type...  62.3 us
    reduce_scatter x1, waiting for transfers between devices, on_device(): lax.psum_scatter(expand_part, 'dp', scatter_dimension=0, tiled=True)  55.5 us
    reduce_scatter x1, waiting for transfers between devices, on_device(): lax.psum_scatter(shrink_part, 'dp', scatter_dimension=0, tiled=True)  52.9 us
    dot_general x8, matrix products, block_inputs(): jnp.einsum('qhd,khd->hqk', query_block, seq_keys, preferred_element_type=...  51.5 us
  transfers between devices with their start and end apart: 15, of which 9 were waited for; matrix products, arithmetic and copies ran while one was open for 45% of the time, Pallas kernels for 0%

commit v1 on v0

v1 whole, which is shorter than its diff:
```python
from functools import partial

import jax
import jax.numpy as jnp
from jax import lax
from jax.experimental import pallas as pl
from jax.experimental.pallas import tpu as pltpu
from jax.sharding import Mesh
from jax.sharding import PartitionSpec as P

HD = 64
ROT = 16
L = 2048
LANES = 128
EPSILON = 1e-05
MASKED = -1e30
AXES = ("pair", "core", "half", "m")
PIECES = 4
PIECE = L // PIECES
SEG_LANE = 64
DOCS = 5
LSE_LANE = SEG_LANE + DOCS
DELTA_LANE = 64
MIB = 1024 * 1024
F32 = jnp.float32
BF16 = jnp.bfloat16


def dot_nn(left, right):
    return lax.dot_general(left, right, (((1,), (0,)), ((), ())), preferred_element_type=F32)


def dot_nt(left, right):
    return lax.dot_general(left, right, (((1,), (1,)), ((), ())), preferred_element_type=F32)


def dot_tn(left, right):
    return lax.dot_general(left, right, (((0,), (0,)), ((), ())), preferred_element_type=F32)


def lanes_of(shape):
    return lax.broadcasted_iota(jnp.int32, shape, len(shape) - 1)


def rows_of(shape):
    return lax.broadcasted_iota(jnp.int32, shape, len(shape) - 2)


def normalize(x):
    rows = x.astype(F32)
    centered = rows - jnp.mean(rows, axis=-1, keepdims=True)
    return centered * lax.rsqrt(jnp.mean(centered * centered, axis=-1, keepdims=True) + EPSILON)


def split3(column):
    high = column.astype(BF16).astype(F32)
    rest = column - high
    middle = rest.astype(BF16).astype(F32)
    return high, middle, rest - middle


def with_lanes(base, first, columns):
    lane = lanes_of(base.shape)
    for offset, column in enumerate(columns):
        base = jnp.where(lane == first + offset, column, base)
    return base


def params(limit_mib):
    return pltpu.CompilerParams(vmem_limit_bytes=limit_mib * MIB)


def whole(shape, **kw):
    return pl.BlockSpec(shape, lambda *_: (0,) * len(shape), **kw)


def once(shape):
    return whole(shape, pipeline_mode=pl.Buffered(1))


def cost(flops, nbytes, trans=0):
    return pl.CostEstimate(flops=int(flops), bytes_accessed=int(nbytes), transcendentals=int(trans))


def row_offsets(info_ref, pairs, rows):
    core, pair = info_ref[1], info_ref[2]
    for j in range(pairs):
        base = (pair ^ j) * 2
        yield pl.multiple_of((base + core) * rows, rows), pl.multiple_of((base + 1 - core) * rows, rows)


def assemble_first_kernel(pairs, rows, width, info_ref, *refs):
    a_refs, b_refs = refs[:pairs], refs[pairs : 2 * pairs]
    weight_ref, gb_ref, small = refs[2 * pairs :]
    for j, (off_a, off_b) in enumerate(row_offsets(info_ref, pairs, rows)):
        for off, part in ((off_a, a_refs[j]), (off_b, b_refs[j])):
            weight_ref[pl.ds(off, rows), :] = part[:, :width]
            small[pl.ds(off, rows), :] = part[:, width:].astype(F32)
    gb_ref[...] = small[...].T[:8, :]


def assemble_first(info, a_parts, b_parts, width):
    pairs, rows = len(a_parts), a_parts[0].shape[0]
    feats = pairs * 2 * rows
    return pl.pallas_call(
        partial(assemble_first_kernel, pairs, rows, width),
        out_shape=(jax.ShapeDtypeStruct((feats, width), BF16), jax.ShapeDtypeStruct((8, feats), F32)),
        in_specs=[pl.BlockSpec(memory_space=pltpu.SMEM)] + [pl.BlockSpec(memory_space=pltpu.VMEM)] * (2 * pairs),
        scratch_shapes=[pltpu.VMEM((feats, LANES), F32)],
        compiler_params=params(32),
        cost_estimate=cost(0, 4 * feats * width),
        name="assemble_qkv",
    )(info, *a_parts, *b_parts)


def assemble_second_kernel(pairs, rows, widths, info_ref, *refs):
    a_refs, b_refs, outs = refs[:pairs], refs[pairs : 2 * pairs], refs[2 * pairs :]
    for j, (off_a, off_b) in enumerate(row_offsets(info_ref, pairs, rows)):
        for off, part in ((off_a, a_refs[j]), (off_b, b_refs[j])):
            start = 0
            for out, width in zip(outs, widths):
                out[pl.ds(off, rows), :] = part[:, start : start + width]
                start += width


def assemble_second(info, a_parts, b_parts, widths):
    pairs, rows = len(a_parts), a_parts[0].shape[0]
    feats = pairs * 2 * rows
    return pl.pallas_call(
        partial(assemble_second_kernel, pairs, rows, widths),
        out_shape=tuple(jax.ShapeDtypeStruct((feats, w), BF16) for w in widths),
        in_specs=[pl.BlockSpec(memory_space=pltpu.SMEM)] + [pl.BlockSpec(memory_space=pltpu.VMEM)] * (2 * pairs),
        compiler_params=params(32),
        cost_estimate=cost(0, 4 * feats * sum(widths)),
        name="assemble_ffn",
    )(info, *a_parts, *b_parts)


def turn(values, cosine, sine_up, sine_down):
    return (
        values * cosine
        + pltpu.roll(values, ROT // 2, 1) * sine_up
        + pltpu.roll(values, LANES - ROT // 2, 1) * sine_down
    )


def project_kernel(heads, info_ref, x_ref, w_ref, gb_ref, cos_ref, up_ref, down_ref, qf_ref, kf_ref, *refs):
    xs_ref, q_ref, k_ref, v_ref = refs[-4:]
    x = x_ref[...]
    xs_ref[0] = x
    first = (normalize(x) * gb_ref[0:1, :] + gb_ref[2:3, :]).astype(BF16)
    projected = dot_nn(first, w_ref[...])
    cosine, up, down = cos_ref[...], up_ref[...], down_ref[...]
    lane = lanes_of(cosine.shape)
    low = lane < HD
    value_feature = ((lane >= DELTA_LANE) & (lane < DELTA_LANE + 3)).astype(F32)

    def part(offset):
        tile = projected[:, offset // LANES * LANES : offset // LANES * LANES + LANES]
        return pltpu.roll(tile, HD, 1) if offset % LANES else tile

    for h in range(heads):
        sl = slice(h * LANES, (h + 1) * LANES)
        base = h * 3 * HD
        query = turn(part(base), cosine, up, down) * HD ** (-0.5)
        key = turn(part(base + HD), cosine, up, down)
        q_ref[0, :, sl] = jnp.where(low, query, qf_ref[...]).astype(BF16)
        k_ref[0, :, sl] = jnp.where(low, key, kf_ref[...]).astype(BF16)
        v_ref[0, :, sl] = jnp.where(low, part(base + 2 * HD), value_feature).astype(BF16)


def project(r, info, x, weight, gb, tables, stacks, block=256):
    feats, width = weight.shape
    heads = width // (3 * HD)
    steps = PIECE // block
    shapes = [(PIECES, PIECE, feats)] + [(PIECES, PIECE, heads * LANES)] * 3
    table = pl.BlockSpec((block, LANES), lambda i, info: ((info[0] ^ r) * steps + i, 0))
    n_fixed = 9
    return pl.pallas_call(
        partial(project_kernel, heads),
        grid_spec=pltpu.PrefetchScalarGridSpec(
            num_scalar_prefetch=1,
            grid=(steps,),
            in_specs=[
                pl.BlockSpec((block, feats), lambda i, info: (i, 0)),
                once((feats, width)),
                once((8, feats)),
            ]
            + [table] * 5
            + [pl.BlockSpec(memory_space=pl.ANY)] * len(stacks),
            out_specs=[pl.BlockSpec((1, block, s[2]), lambda i, info: (r, i, 0)) for s in shapes],
        ),
        out_shape=[jax.ShapeDtypeStruct(s, BF16) for s in shapes],
        input_output_aliases={n_fixed + n: n for n in range(len(stacks))},
        compiler_params=params(40),
        cost_estimate=cost(2 * PIECE * feats * width, 2 * (feats * width + 4 * PIECE * feats)),
        name=f"project_piece_{r}",
    )(info, x, weight, gb, *tables, *stacks)


def attend_kernel(heads, block, info_ref, q_ref, k_ref, v_ref, o_ref, qb_ref):
    step = pl.program_id(0)
    per = PIECE // block
    me = info_ref[0]

    def run(count):
        row = step % per * block + rows_of((block, PIECE))
        causal = lanes_of((block, PIECE)) <= row
        lane = lanes_of((block, LANES))
        pieces = [me ^ j for j in range(count)]
        held = None
        for h in range(heads):
            sl = slice(h * LANES, (h + 1) * LANES)
            query = q_ref[:, sl]
            scores = [dot_nt(query, k_ref[p, :, sl]) for p in pieces]
            scores[-1] = jnp.where(causal, scores[-1], MASKED)
            top = jnp.max(scores[0], axis=-1, keepdims=True)
            for s in scores[1:]:
                top = jnp.maximum(top, jnp.max(s, axis=-1, keepdims=True))
            weights = [jnp.exp(s - top) for s in scores]
            total = jnp.sum(weights[0], axis=-1, keepdims=True)
            for w in weights[1:]:
                total = total + jnp.sum(w, axis=-1, keepdims=True)
            scale = 1.0 / total
            out = None
            for w, p in zip(weights, pieces):
                term = dot_nn((w * scale).astype(BF16), v_ref[p, :, sl])
                out = term if out is None else out + term
            if h % 2 == 0:
                held = out
            else:
                o_ref[:, (h // 2) * LANES : (h // 2 + 1) * LANES] = jnp.where(
                    lane < HD, held, pltpu.roll(out, HD, 1)
                )
            log_total = split3(top + jnp.log(total))
            qb_ref[:, sl] = with_lanes(query.astype(F32), LSE_LANE, [-c for c in log_total]).astype(BF16)

    for n in range(PIECES):
        pl.when(step // per == n)(partial(run, n + 1))


def attend(info, queries, keys, values, block=256):
    width = queries.shape[2]
    heads = width // LANES
    per = PIECE // block
    rel = lambda i, info: ((info[0] ^ (i // per)) * per + i % per, 0)
    return pl.pallas_call(
        partial(attend_kernel, heads, block),
        grid_spec=pltpu.PrefetchScalarGridSpec(
            num_scalar_prefetch=1,
            grid=(L // block,),
            in_specs=[
                pl.BlockSpec((block, width), rel),
                once((PIECES, PIECE, width)),
                once((PIECES, PIECE, width)),
            ],
            out_specs=[pl.BlockSpec((block, heads * HD), rel), pl.BlockSpec((block, width), rel)],
        ),
        out_shape=[jax.ShapeDtypeStruct((L, heads * HD), F32), jax.ShapeDtypeStruct((L, width), BF16)],
        compiler_params=params(50),
        cost_estimate=cost(heads * L * L * LANES * 4, 5 * L * width, heads * L * L // 2),
        name="attention_forward",
    )(info, queries.reshape(L, width), keys, values)


def gelu_parts(h):
    bell = jnp.exp(h * h * -0.5)
    t = 1.0 / (1.0 + (0.3275911 * 0.5**0.5) * jnp.abs(h))
    poly = t * (
        0.254829592 + t * (-0.284496736 + t * (1.421413741 + t * (-1.453152027 + t * 1.061405429)))
    )
    tail = 0.5 * poly * bell
    return jnp.where(h < 0, tail, 1.0 - tail), bell * 0.3989422804014327


def norm_columns(sums_ref):
    wide = jnp.concatenate([sums_ref[...], jnp.zeros((LANES - 8, sums_ref.shape[1]), F32)], axis=0)
    return wide.T


def write_parts(info_ref, totals, width, small, a_refs, b_refs):
    rows = a_refs[0].shape[0]
    for j, (off_a, off_b) in enumerate(row_offsets(info_ref, len(a_refs), rows)):
        for off, part in ((off_a, a_refs[j]), (off_b, b_refs[j])):
            start = 0
            for total in totals:
                part[:, start : start + total.shape[1]] = total[pl.ds(off, rows), :].astype(BF16)
                start += total.shape[1]
            part[:, width:] = small[pl.ds(off, rows), :].astype(BF16)


def feed_kernel(pairs, heads, info_ref, x_ref, *refs):
    g_refs = refs[:PIECES]
    o_ref, wd_ref, we_ref, ws_ref, gb_ref = refs[PIECES : PIECES + 5]
    outs = refs[PIECES + 5 :]
    br_refs = outs[:PIECES]
    sg_ref, doa_ref = outs[PIECES : PIECES + 2]
    a_refs = outs[PIECES + 2 : PIECES + 2 + pairs]
    b_refs = outs[PIECES + 2 + pairs : PIECES + 2 + 2 * pairs]
    g_now, b_now, gd, ge, gs, sums, small = outs[PIECES + 2 + 2 * pairs :]
    step, last = pl.program_id(0), pl.num_programs(0) - 1
    block = x_ref.shape[0]
    per = PIECE // block

    @pl.when(step == 0)
    def _():
        for total in (gd, ge, gs, sums):
            total[...] = jnp.zeros_like(total)

    place = pl.multiple_of(step % per * block, block)
    for r in range(PIECES):

        @pl.when(step // per == r)
        def _():
            g_now[...] = g_refs[r][pl.ds(place, block), :]

    g = g_now[...]
    normalized = normalize(x_ref[...])
    second = (normalized * gb_ref[1:2, :] + gb_ref[3:4, :]).astype(BF16)
    hidden = dot_nn(second, we_ref[...])
    cdf, density = gelu_parts(hidden)
    activated = (hidden * cdf).astype(BF16)
    slope = cdf + hidden * density
    out = o_ref[...]
    attended = out.astype(BF16)
    b_now[...] = (dot_nt(attended, wd_ref[...]) + dot_nt(activated, ws_ref[...])).astype(BF16)
    hidden_grad = (dot_nn(g, ws_ref[...]) * slope).astype(BF16)
    second_grad = dot_nt(hidden_grad, we_ref[...])
    sg_ref[...] = second_grad * gb_ref[1:2, :]
    sums[0:1, :] += jnp.sum(second_grad * normalized, axis=0, keepdims=True)
    sums[1:2, :] += jnp.sum(second_grad, axis=0, keepdims=True)
    ge[...] += dot_tn(second, hidden_grad)
    gs[...] += dot_tn(g, activated)
    gd[...] += dot_tn(g, attended)
    attended_grad = dot_nn(g, wd_ref[...]).astype(BF16).astype(F32)
    product = attended_grad * out
    lane = lanes_of((block, LANES))
    for h in range(heads):
        tile = slice(h // 2 * LANES, (h // 2 + 1) * LANES)
        mine = (lane < HD) if h % 2 == 0 else (lane >= HD)
        delta = split3(jnp.sum(jnp.where(mine, product[:, tile], 0.0), axis=-1, keepdims=True))
        grad = attended_grad[:, tile]
        if h % 2:
            grad = pltpu.roll(grad, HD, 1)
        grad = jnp.where(lane < HD, grad, 0.0)
        doa_ref[:, h * LANES : (h + 1) * LANES] = with_lanes(grad, DELTA_LANE, [-c for c in delta]).astype(BF16)
    for r in range(PIECES):

        @pl.when(step // per == r)
        def _():
            br_refs[r][pl.ds(place, block), :] = b_now[...]

    @pl.when(step == last)
    def _():
        small[...] = norm_columns(sums)
        width = sum(t.shape[1] for t in (gd, ge, gs))
        write_parts(info_ref, (gd, ge, gs), width, small, a_refs, b_refs)


def feed(info, xs, g_parts, out, wd, we, ws, gb, pairs, block=256):
    feats, hidden = we.shape
    heads = wd.shape[1] // HD
    rows = feats // (2 * pairs)
    width = wd.shape[1] + 2 * hidden
    piece = (PIECE, feats)
    part = (rows, width + LANES)
    by_step = lambda i: (i, 0)
    return pl.pallas_call(
        partial(feed_kernel, pairs, heads),
        grid=(L // block,),
        in_specs=[pl.BlockSpec(memory_space=pltpu.SMEM), pl.BlockSpec((block, feats), by_step)]
        + [once(piece)] * PIECES
        + [pl.BlockSpec((block, heads * HD), by_step)]
        + [once(wd.shape), once(we.shape), once(ws.shape), once(gb.shape)],
        out_specs=[once(piece)] * PIECES
        + [pl.BlockSpec((block, feats), by_step), pl.BlockSpec((block, heads * LANES), by_step)]
        + [once(part)] * (2 * pairs),
        out_shape=[jax.ShapeDtypeStruct(piece, BF16)] * PIECES
        + [jax.ShapeDtypeStruct((L, feats), F32), jax.ShapeDtypeStruct((L, heads * LANES), BF16)]
        + [jax.ShapeDtypeStruct(part, BF16)] * (2 * pairs),
        scratch_shapes=[
            pltpu.VMEM((block, feats), BF16),
            pltpu.VMEM((block, feats), BF16),
            pltpu.VMEM(wd.shape, F32),
            pltpu.VMEM(we.shape, F32),
            pltpu.VMEM(ws.shape, F32),
            pltpu.VMEM((8, feats), F32),
            pltpu.VMEM((feats, LANES), F32),
        ],
        compiler_params=params(60),
        cost_estimate=cost(12 * L * feats * hidden, 20 * L * feats),
        name="feed_forward_and_back",
    )(info, xs.reshape(L, feats), *g_parts, out, wd, we, ws, gb)


def attend_back_kernel(info_ref, q_ref, do_ref, k_ref, v_ref, cos_ref, up_ref, down_ref, pg_ref, dq, dk, dv):
    me = info_ref[0]
    here = q_ref.shape[1] // LANES
    causal = rows_of((PIECE, PIECE)) <= lanes_of((PIECE, PIECE))
    at = [pl.multiple_of((me ^ j) * PIECE, PIECE) for j in range(PIECES)]
    for h in range(here):
        sl = slice(h * LANES, (h + 1) * LANES)
        for j in range(PIECES):
            key = k_ref[pl.ds(at[j], PIECE), sl]
            value = v_ref[pl.ds(at[j], PIECE), sl]
            key_sum = value_sum = None
            for i in range(j, PIECES):
                query = q_ref[pl.ds(at[i], PIECE), sl]
                grad = do_ref[pl.ds(at[i], PIECE), sl]
                scores = dot_nt(key, query)
                if i == j:
                    scores = jnp.where(causal, scores, MASKED)
                probs = jnp.exp(scores)
                score_grad = (probs * dot_nt(value, grad)).astype(BF16)
                value_term = dot_nn(probs.astype(BF16), grad)
                key_term = dot_nn(score_grad, query)
                value_sum = value_term if value_sum is None else value_sum + value_term
                key_sum = key_term if key_sum is None else key_sum + key_term
                query_term = dot_tn(score_grad, key)
                if j == 0:
                    dq[h, i] = query_term
                else:
                    dq[h, i] += query_term
            dk[h, j] = key_sum
            dv[h, j] = value_sum
    low = lanes_of((PIECE, LANES)) < HD

    def join(left, right):
        return jnp.where(low, left, pltpu.roll(right, HD, 1)).astype(BF16)

    for j in range(PIECES):
        rows = pl.ds(at[j], PIECE)
        cosine = cos_ref[j * PIECE : (j + 1) * PIECE, :]
        up, down = -up_ref[j * PIECE : (j + 1) * PIECE, :], -down_ref[j * PIECE : (j + 1) * PIECE, :]
        for h in range(0, here, 2):
            start = h // 2 * 3 * LANES
            q0, q1 = (turn(dq[h + n, j] * HD ** (-0.5), cosine, up, down) for n in (0, 1))
            k0, k1 = (turn(dk[h + n, j], cosine, up, down) for n in (0, 1))
            v0, v1 = dv[h, j], dv[h + 1, j]
            for n, (left, right) in enumerate(((q0, k0), (v0, q1), (k1, v1))):
                pg_ref[rows, start + n * LANES : start + (n + 1) * LANES] = join(left, right)


def attend_back(info, queries, grads, keys, values, tables, group=2):
    width = queries.shape[1]
    heads = width // LANES
    head_block = pl.BlockSpec((L, group * LANES), lambda s, info: (0, s))
    table = once((L, LANES))
    return pl.pallas_call(
        attend_back_kernel,
        grid_spec=pltpu.PrefetchScalarGridSpec(
            num_scalar_prefetch=1,
            grid=(heads // group,),
            in_specs=[head_block] * 4 + [table] * 3,
            out_specs=pl.BlockSpec((L, group * 3 * HD), lambda s, info: (0, s)),
            scratch_shapes=[pltpu.VMEM((group, PIECES, PIECE, LANES), F32)] * 3,
        ),
        out_shape=jax.ShapeDtypeStruct((L, heads * 3 * HD), BF16),
        compiler_params=params(60),
        cost_estimate=cost(10 * heads * L * L * LANES, 12 * L * width, heads * L * L // 2),
        name="attention_backward",
    )(info, queries, grads, keys.reshape(L, width), values.reshape(L, width), *tables)


def project_back_kernel(pairs, info_ref, pg_ref, x_ref, sg_ref, w_ref, gb_ref, *refs):
    e_refs = refs[:PIECES]
    a_refs, b_refs = refs[PIECES : PIECES + pairs], refs[PIECES + pairs : PIECES + 2 * pairs]
    e_now, gq, sums, small = refs[PIECES + 2 * pairs :]
    step, last = pl.program_id(0), pl.num_programs(0) - 1
    block = x_ref.shape[0]
    per = PIECE // block

    @pl.when(step == 0)
    def _():
        gq[...] = jnp.zeros_like(gq)
        sums[...] = jnp.zeros_like(sums)

    normalized = normalize(x_ref[...])
    first = (normalized * gb_ref[0:1, :] + gb_ref[2:3, :]).astype(BF16)
    grad = pg_ref[...]
    first_grad = dot_nt(grad, w_ref[...])
    gq[...] += dot_tn(first, grad)
    e_now[...] = (first_grad * gb_ref[0:1, :] + sg_ref[...]).astype(BF16)
    sums[0:1, :] += jnp.sum(first_grad * normalized, axis=0, keepdims=True)
    sums[1:2, :] += jnp.sum(first_grad, axis=0, keepdims=True)
    place = pl.multiple_of(step % per * block, block)
    for r in range(PIECES):

        @pl.when(step // per == r)
        def _():
            e_refs[r][pl.ds(place, block), :] = e_now[...]

    @pl.when(step == last)
    def _():
        small[...] = norm_columns(sums)
        write_parts(info_ref, (gq,), gq.shape[1], small, a_refs, b_refs)


def project_back(info, pg, xs, sg, weight, gb, pairs, block=256):
    feats, width = weight.shape
    rows = feats // (2 * pairs)
    piece, part = (PIECE, feats), (rows, width + LANES)
    by_step = lambda i: (i, 0)
    return pl.pallas_call(
        partial(project_back_kernel, pairs),
        grid=(L // block,),
        in_specs=[
            pl.BlockSpec(memory_space=pltpu.SMEM),
            pl.BlockSpec((block, width), by_step),
            pl.BlockSpec((block, feats), by_step),
            pl.BlockSpec((block, feats), by_step),
            once(weight.shape),
            once(gb.shape),
        ],
        out_specs=[once(piece)] * PIECES + [once(part)] * (2 * pairs),
        out_shape=[jax.ShapeDtypeStruct(piece, BF16)] * PIECES
        + [jax.ShapeDtypeStruct(part, BF16)] * (2 * pairs),
        scratch_shapes=[
            pltpu.VMEM((block, feats), BF16),
            pltpu.VMEM(weight.shape, F32),
            pltpu.VMEM((8, feats), F32),
            pltpu.VMEM((feats, LANES), F32),
        ],
        compiler_params=params(50),
        cost_estimate=cost(4 * L * feats * width, 10 * L * feats),
        name="project_back",
    )(info, pg, xs.reshape(L, feats), sg, weight, gb)


def build_tables(segments):
    places = jnp.arange(L, dtype=jnp.int32)
    starts = jnp.zeros_like(segments)
    for value in range(DOCS):
        starts = starts + jnp.where(segments > value, jnp.sum((segments == value).astype(jnp.int32)), 0)
    position = (places - starts).astype(F32)
    lane = jnp.arange(LANES, dtype=jnp.int32)
    inner = lane % HD
    half = ROT // 2
    frequency = 10000.0 ** (-((inner % half).astype(F32) * 2.0 / ROT))
    angles = position[:, None] * frequency[None, :]
    turned = (inner < ROT)[None, :]
    sine = jnp.sin(angles)
    cosine = jnp.where(turned, jnp.cos(angles), 1.0)
    up = jnp.where(turned & (inner >= half)[None, :], sine, 0.0)
    down = jnp.where((inner < half)[None, :], -sine, 0.0)
    feature = lane - SEG_LANE
    is_doc = ((feature >= 0) & (feature < DOCS))[None, :]
    same = segments[:, None] == feature[None, :]
    one = ((lane >= LSE_LANE) & (lane < LSE_LANE + 3))[None, :]
    query_feature = jnp.where(is_doc & ~same, MASKED, 0.0)
    key_feature = jnp.where((is_doc & same) | one, 1.0, 0.0)
    return cosine, up, down, query_feature, key_feature


class Wires:
    def __init__(self, mesh):
        self.pairs = mesh.shape["pair"]
        self.sizes = [mesh.shape[a] for a in AXES]

    def send(self, array, target):
        _, cores, halves, ms = self.sizes

        def index(k, c, h, m):
            return ((k * cores + c) * halves + h) * ms + m

        moves = []
        for k in range(self.pairs):
            for c in range(cores):
                for h in range(halves):
                    for m in range(ms):
                        there = target(k, c, h, m)
                        if there is not None:
                            moves.append((index(k, c, h, m), index(*there)))
        return lax.ppermute(array, AXES, moves)

    def core(self, array):
        return self.send(array, lambda k, c, h, m: (k, 1 - c, h, m))

    def near(self, array):
        return self.send(array, lambda k, c, h, m: (k, c, h, 1 - m))

    def half(self, array):
        return self.send(array, lambda k, c, h, m: (k, c, 1 - h, m))

    def regroup(self, array):
        return self.send(array, lambda k, c, h, m: (k, 1 - c, 1 - h, m) if c != h else None)

    def plane(self, array, bit):
        return self.send(array, lambda k, c, h, m: (k ^ bit, c, h, m))

    def bits(self):
        bits = [1 << b for b in range(self.pairs.bit_length() - 1)]
        return bits, bits[::-1]

    def plane_gather(self, a_block, b_block):
        result = []
        for block, bits in zip((a_block, b_block), self.bits()):
            parts = {0: block}
            for bit in bits:
                for j in list(parts):
                    parts[j | bit] = self.plane(parts[j], bit)
            result.append([parts[j] for j in range(self.pairs)])
        return result

    def plane_scatter(self, a_parts, b_parts):
        result = []
        for parts, bits in zip((a_parts, b_parts), self.bits()):
            parts = dict(enumerate(parts))
            for bit in reversed(bits):
                for j in sorted(j for j in parts if j & bit):
                    arrived = self.plane(parts.pop(j), bit).astype(F32)
                    parts[j ^ bit] = (parts[j ^ bit].astype(F32) + arrived).astype(BF16)
            result.append(parts[0])
        return result


def on_device(mesh, inputs, qkv_weight, dense_weight, expand_weight, shrink_weight, norm_gains, norm_biases, cotangent, segments):
    wires = Wires(mesh)
    pairs = wires.pairs
    pair, core, half, near = (lax.axis_index(a) for a in AXES)
    native = core == half
    me = 2 * core + near
    info = jnp.stack([me, core, pair, half]).astype(jnp.int32)
    rows = qkv_weight.shape[0]

    def gather_weights(block):
        swapped = wires.half(block)
        own = jnp.where(native, block, swapped)
        other = wires.core(jnp.where(native, swapped, block))
        return wires.plane_gather(own, other)

    def gather_tokens(block):
        mine = jnp.where(native, block, wires.regroup(block))
        beside = wires.near(mine)
        return mine, beside, wires.core(mine), wires.core(beside)

    def reduce_tokens(parts):
        kept = parts[0].astype(F32) + wires.core(parts[2]).astype(F32)
        passed = (parts[1].astype(F32) + wires.core(parts[3]).astype(F32)).astype(BF16)
        kept = kept + wires.near(passed).astype(F32)
        return jnp.where(native, kept, wires.regroup(kept.astype(BF16)).astype(F32))

    def reduce_weights(a_parts, b_parts):
        a_sum, b_sum = wires.plane_scatter(a_parts, b_parts)
        other = wires.core(b_sum)
        mine = jnp.where(native, a_sum, other).astype(F32)
        sent = jnp.where(native, other, a_sum)
        arrived = wires.half(sent).astype(F32)
        total = mine + arrived
        small = (a_sum[:, -LANES:].astype(F32) + other[:, -LANES:].astype(F32)).astype(BF16)
        small = small.astype(F32) + wires.half(small).astype(F32)
        small = small + wires.near(small.astype(BF16)).astype(F32)
        return total[:, :-LANES], small[:, :2].T

    small = jnp.concatenate([norm_gains, norm_biases], axis=0).T
    first_block = jnp.concatenate([qkv_weight, jnp.pad(small, ((0, 0), (0, LANES - 4)))], axis=1)
    first_parts = gather_weights(first_block)
    x_parts = gather_tokens(inputs)
    other_segments = wires.core(segments)
    tables = build_tables(jnp.where(native, segments, other_segments))
    second_parts = gather_weights(jnp.concatenate([dense_weight, expand_weight, shrink_weight], axis=1))
    g_parts = gather_tokens(cotangent)

    qkv_full, gb = assemble_first(info, *first_parts, qkv_weight.shape[1])
    stacks = ()
    for r in range(PIECES):
        stacks = project(r, info, x_parts[r], qkv_full, gb, tables, stacks)
    xs, queries, keys, values = stacks
    out, queries_back = attend(info, queries, keys, values)
    widths = (dense_weight.shape[1], expand_weight.shape[1], shrink_weight.shape[1])
    dense_full, expand_full, shrink_full = assemble_second(info, *second_parts, widths)
    results = feed(info, xs, g_parts, out, dense_full, expand_full, shrink_full, gb, pairs)
    branches = results[:PIECES]
    second_e, out_grads = results[PIECES : PIECES + 2]
    feed_grads = results[PIECES + 2 : PIECES + 2 + pairs], results[PIECES + 2 + pairs :]
    rows_f32 = inputs.astype(F32)
    layer_out = (rows_f32 + reduce_tokens(branches)).astype(BF16)
    feed_total, feedforward_norm_grad = reduce_weights(*feed_grads)
    dense_grad = feed_total[:, : widths[0]]
    expand_grad = feed_total[:, widths[0] : widths[0] + widths[1]]
    shrink_grad = feed_total[:, widths[0] + widths[1] :]

    projected_grad = attend_back(info, queries_back, out_grads, keys, values, tables[:3])
    results = project_back(info, projected_grad, xs, second_e, qkv_full, gb, pairs)
    e = reduce_tokens(results[:PIECES])
    qkv_grad, attention_norm_grad = reduce_weights(results[PIECES : PIECES + pairs], results[PIECES + pairs :])

    centered = rows_f32 - jnp.mean(rows_f32, axis=-1, keepdims=True)
    inv_scale = lax.rsqrt(jnp.mean(centered * centered, axis=-1, keepdims=True) + EPSILON)
    normalized = centered * inv_scale
    input_grad = cotangent.astype(F32) + inv_scale * (
        e - jnp.mean(e, axis=-1, keepdims=True) - normalized * jnp.mean(e * normalized, axis=-1, keepdims=True)
    )
    return (
        layer_out,
        input_grad,
        qkv_grad,
        dense_grad,
        expand_grad,
        shrink_grad,
        attention_norm_grad,
        feedforward_norm_grad,
    )


def solution(mesh):
    dp, tensor = mesh.shape["dp"], mesh.shape["tensor"]
    fine = Mesh(mesh.devices.reshape(dp // 2, 2, 2, tensor // 2), AXES)
    data, split = ("pair", "core"), ("half", "m")
    tokens, weight, norm = P(AXES, None), P(data, split), P(None, data)
    return jax.shard_map(
        partial(on_device, fine),
        mesh=fine,
        in_specs=(tokens, weight, weight, weight, weight, norm, norm, tokens, P(data)),
        out_specs=(tokens, tokens, weight, weight, weight, weight, norm, norm),
        check_vma=False,
    )
```

time: 1010 us -> 499 us (0.49)
  the two profiles are of different devices: /device:TPU:0 before, /device:TPU:1 now
where the time goes in v1:
time: 499 us; the launch traced here: 492 us
  waiting for transfers between devices  203 us (41%)
  Pallas kernels  150 us (30%)
  starting transfers between devices  87.6 us (18%)
  other arithmetic  33.9 us (7%)
  local copies, waits for them, and re-layouts  16.1 us (3%)
    ppermute x53, waiting for transfers between devices, send(): return lax.ppermute(array, AXES, moves)  203 us
    ppermute x53, starting transfers between devices, send(): return lax.ppermute(array, AXES, moves)  87.6 us
    pallas_call x1, Pallas kernels, feed(): pl.pallas_call(partial(feed_kernel, pairs, heads), grid=(L // block,), in...  51.1 us
    pallas_call x1, Pallas kernels, attend_back(): pl.pallas_call(attend_back_kernel, grid_spec=pltpu.PrefetchScalarGridSpec...  36.5 us
    pallas_call x1, Pallas kernels, attend(): pl.pallas_call(partial(attend_kernel, heads, block), grid_spec=pltpu.Pref...  29.9 us
    pallas_call x4, Pallas kernels, project(): pl.pallas_call(partial(project_kernel, heads), grid_spec=pltpu.PrefetchSc...  16 us
    pallas_call x1, Pallas kernels, project_back(): pl.pallas_call(partial(project_back_kernel, pairs), grid=(L // block,), i...  15 us
    unnamed x82, local copies, waits for them, and re-layouts  12.5 us
  transfers between devices with their start and end apart: 53, of which 17 were waited for; matrix products, arithmetic and copies ran while one was open for 7% of the time, Pallas kernels for 10%

profile of v1, /device:TPU:1, one launch (start us, length us, event | category | flops | bytes accessed | tf_op | source)
XLA Modules:
  0.0 492.1 jit_solution(11158821221686725370)
XLA Ops:
  3.2 3.1 collective-permute-start.3
  14.3 26.4 %collective-permute-done.3 = bf16[128,896]{1,0:T(8,128)(2,1)} collective-permute-done((bf16[128,896]{1,0:T(8,128)(2,1)}, bf16[128,896]{1,0:T(8,128)(2,1)}, u32[]{:S(2)}, u32[]{:S(2)}) %collective-permute-start.3) | collective-permute-done | bytes 229408 | tf_op jit(solution)/shard_map/ppermute | solution.py:574
  44.1 14.7 %collective-permute-done = bf16[512,1024]{1,0:T(8,128)(2,1)S(1)} collective-permute-done((bf16[512,1024]{1,0:T(8,128)(2,1)}, bf16[512,1024]{1,0:T(8,128)(2,1)S(1)}, u32[]{:S(2)}, u32[]{:S(2)}) %collective-permute-start) | collective-permute-done | bytes 1048608 | tf_op jit(solution)/shard_map/ppermute | solution.py:574
  63.7 10.7 %collective-permute-start.1 = (bf16[512,1024]{1,0:T(8,128)(2,1)S(1)}, bf16[512,1024]{1,0:T(8,128)(2,1)S(1)}, u32[]{:S(2)}, u32[]{:S(2)}) collective-permute-start(bf16[512,1024]{1,0:T(8,128)(2,1)S(1)} %broadcast_select_fusion.1.x_ref), channel_id=1, source_target_pairs={{0,1},{1,0},{2,3},{3,2},{4,5},{5,4},{6,7},{7,6},{8,9},{9,8},{10,11... | collective-permute-start | bytes 3145736 | tf_op jit(solution)/shard_map/ppermute | solution.py:574
  78.9 8.7 %collective-permute-done.13 = bf16[512,1024]{1,0:T(8,128)(2,1)S(1)} collective-permute-done((bf16[512,1024]{1,0:T(8,128)(2,1)S(1)}, bf16[512,1024]{1,0:T(8,128)(2,1)S(1)}, u32[]{:S(2)}, u32[]{:S(2)}) %collective-permute-start.13) | collective-permute-done | bytes 1048608 | tf_op jit(solution)/shard_map/ppermute | solution.py:574
  94.7 3.2 subtract_convert_fusion
  98.0 9.0 %collective-permute-done.1.x_ref = bf16[512,1024]{1,0:T(8,128)(2,1)S(1)} collective-permute-done((bf16[512,1024]{1,0:T(8,128)(2,1)S(1)}, bf16[512,1024]{1,0:T(8,128)(2,1)S(1)}, u32[]{:S(2)}, u32[]{:S(2)}) %collective-permute-start.1) | collective-permute-done | bytes 1048608 | tf_op jit(solution)/shard_map/ppermute | solution.py:574
  106.9 3.8 fusion.14
  112.2 7.7 %collective-permute-done.20.refs_3_ = bf16[128,2304]{1,0:T(8,128)(2,1)S(1)} collective-permute-done((bf16[128,2304]{1,0:T(8,128)(2,1)S(1)}, bf16[128,2304]{1,0:T(8,128)(2,1)S(1)}, u32[]{:S(2)}, u32[]{:S(2)}) %collective-permute-start.20) | collective-permute-done | bytes 589856 | tf_op jit(solution)/shard_map/ppermute | solution.py:574
  124.6 4.2 project_piece_0.1
  128.7 3.9 project_piece_1.1
  132.7 3.9 project_piece_2.1
  141.5 3.9 project_piece_3.1
  149.4 29.9 %attention_forward.1 = (f32[2048,256]{1,0:T(8,128)S(1)}, bf16[2048,512]{1,0:T(8,128)(2,1)}) custom-call(s32[4]{0:T(128)S(1)} %pad_add_fusion.info_ref, bf16[2048,512]{1,0:T(8,128)(2,1)} %bitcast.13, bf16[4,512,512]{2,1,0:T(8,128)(2,1)} %copy-done.5, bf16[4,512,512]{2,1,0:T(8,128)(2,1)} %copy-done.6), custom_call_target="tpu_custom_call" | custom-call | flops 8589934592 | bytes 5242880 | tf_op jit(solution)/shard_map/attention_forward/pallas_call | solution.py:247
  180.6 51.1 %feed_forward_and_back.1 = (bf16[512,1024]{1,0:T(8,128)(2,1)}, bf16[512,1024]{1,0:T(8,128)(2,1)}, bf16[512,1024]{1,0:T(8,128)(2,1)}, bf16[512,1024]{1,0:T(8,128)...) custom-call(s32[4]{0:T(128)} %copy-done.9, ...), custom_call_target="tpu_custom_call" | custom-call | flops 25769803776 | bytes 41943040 | tf_op jit(solution)/shard_map/feed_forward_and_back/pallas_call | solution.py:368
  231.8 36.5 %attention_backward.1.pg_ref = bf16[2048,768]{1,0:T(8,128)(2,1)} custom-call(s32[4]{0:T(128)} %copy-done.9, bf16[2048,512]{1,0:T(8,128)(2,1)} %get-tuple-element.83.q_ref, bf16[2048,512]{1,0:T(8,128)(2,1)} %get-tuple-element.84.do_ref, bf16[2048,512]{1,0:T(8,128)(2,1)} %bitcast.14, bf16[2048,512]{1,0:T(8,128)(2,1)} %bitcast.15, f32[2048,128]{1,0:T(8,128)} %copy-done.2, ...), custom_call_target="tpu_custom_call" | custom-call | flops 21474836480 | bytes 12582912 | tf_op jit(solution)/shard_map/attention_backward/pallas_call | solution.py:449
  268.3 15.0 %project_back.1 = (bf16[512,1024]{1,0:T(8,128)(2,1)S(1)}, bf16[512,1024]{1,0:T(8,128)(2,1)S(1)}, bf16[512,1024]{1,0:T(8,128)(2,1)}, bf16[512,1024]{1,0:T(8,128)(...) custom-call(s32[4]{0:T(128)S(1)} %copy-done.10, ...), custom_call_target="tpu_custom_call" | custom-call | flops 6442450944 | bytes 20971520 | tf_op jit(solution)/shard_map/project_back/pallas_call | solution.py:504
  290.6 13.5 %collective-permute-done.34 = bf16[128,896]{1,0:T(8,128)(2,1)S(1)} collective-permute-done((bf16[128,896]{1,0:T(8,128)(2,1)S(1)}, bf16[128,896]{1,0:T(8,128)(2,1)S(1)}, u32[]{:S(2)}, u32[]{:S(2)}) %collective-permute-start.34) | collective-permute-done | bytes 229408 | tf_op jit(solution)/shard_map/ppermute | solution.py:574
  305.4 15.4 %collective-permute-done.36 = bf16[128,896]{1,0:T(8,128)(2,1)S(1)} collective-permute-done((bf16[128,896]{1,0:T(8,128)(2,1)S(1)}, bf16[128,896]{1,0:T(8,128)(2,1)S(1)}, u32[]{:S(2)}, u32[]{:S(2)}) %collective-permute-start.36) | collective-permute-done | bytes 229408 | tf_op jit(solution)/shard_map/ppermute | solution.py:574
  337.4 4.8 collective-permute-done.46
  345.8 9.8 %collective-permute-done.41 = bf16[128,2432]{1,0:T(8,128)(2,1)S(1)} collective-permute-done((bf16[128,2432]{1,0:T(8,128)(2,1)S(1)}, bf16[128,2432]{1,0:T(8,128)(2,1)S(1)}, u32[]{:S(2)}, u32[]{:S(2)}) %collective-permute-start.41) | collective-permute-done | bytes 622624 | tf_op jit(solution)/shard_map/ppermute | solution.py:574
  359.1 4.0 collective-permute-start.51
  364.6 16.5 %collective-permute-done.51 = bf16[128,128]{1,0:T(8,128)(2,1)S(1)} collective-permute-done((bf16[128,128]{1,0:T(8,128)(2,1)S(1)}, bf16[128,128]{1,0:T(8,128)(2,1)S(1)}, u32[]{:S(2)}, u32[]{:S(2)}) %collective-permute-start.51) | collective-permute-done | bytes 32800 | tf_op jit(solution)/shard_map/ppermute | solution.py:574
  381.1 5.8 %collective-permute-start.27 = (bf16[512,1024]{1,0:T(8,128)(2,1)}, bf16[512,1024]{1,0:T(8,128)(2,1)}, u32[]{:S(2)}, u32[]{:S(2)}) collective-permute-start(bf16[512,1024]{1,0:T(8,128)(2,1)} %add_convert_fusion.1), channel_id=1, source_target_pairs={{0,1},{1,0},{2,3},{3,2},{4,5},{5,4},{6,7},{7,6},{8,9},{9,8},{10,11... | collective-permute-start | bytes 3145736 | tf_op jit(solution)/shard_map/ppermute | solution.py:574
  387.6 4.6 collective-permute-start.52
  394.1 15.3 %collective-permute-done.52 = bf16[128,128]{1,0:T(8,128)(2,1)S(1)} collective-permute-done((bf16[128,128]{1,0:T(8,128)(2,1)S(1)}, bf16[128,128]{1,0:T(8,128)(2,1)S(1)}, u32[]{:S(2)}, u32[]{:S(2)}) %collective-permute-start.52) | collective-permute-done | bytes 32800 | tf_op jit(solution)/shard_map/ppermute | solution.py:574
  409.3 6.1 %collective-permute-start.48 = (bf16[128,2432]{1,0:T(8,128)(2,1)}, bf16[128,2432]{1,0:T(8,128)(2,1)}, u32[]{:S(2)}, u32[]{:S(2)}) collective-permute-start(bf16[128,2432]{1,0:T(8,128)(2,1)} %get-tuple-element.129), channel_id=1, source_target_pairs={{0,2},{1,3},{2,0},{3,1},{4,6},{5,7},{6,4},{7,5},{8,10},{9,11},{10,... | collective-permute-start | bytes 1867784 | tf_op jit(solution)/shard_map/ppermute | solution.py:574
  423.1 3.7 collective-permute-start.28
  426.8 38.7 %collective-permute-done.48 = bf16[128,2432]{1,0:T(8,128)(2,1)} collective-permute-done((bf16[128,2432]{1,0:T(8,128)(2,1)}, bf16[128,2432]{1,0:T(8,128)(2,1)}, u32[]{:S(2)}, u32[]{:S(2)}) %collective-permute-start.48) | collective-permute-done | bytes 622624 | tf_op jit(solution)/shard_map/ppermute | solution.py:574
  468.6 8.4 %collective-permute-done.32 = bf16[512,1024]{1,0:T(8,128)(2,1)S(1)} collective-permute-done((bf16[512,1024]{1,0:T(8,128)(2,1)S(1)}, bf16[512,1024]{1,0:T(8,128)(2,1)S(1)}, u32[]{:S(2)}, u32[]{:S(2)}) %collective-permute-start.32) | collective-permute-done | bytes 1048608 | tf_op jit(solution)/shard_map/ppermute | solution.py:574
  479.5 8.6 %collective-permute-done.28 = bf16[512,1024]{1,0:T(8,128)(2,1)S(1)} collective-permute-done((bf16[512,1024]{1,0:T(8,128)(2,1)S(1)}, bf16[512,1024]{1,0:T(8,128)(2,1)S(1)}, u32[]{:S(2)}, u32[]{:S(2)}) %collective-permute-start.28) | collective-permute-done | bytes 1048608 | tf_op jit(solution)/shard_map/ppermute | solution.py:574
  488.2 3.6 fusion.7
  (214 shorter events, 95.8 us)
Async XLA Ops:
  3.2 37.6 %collective-permute-start.3 = (bf16[128,896]{1,0:T(8,128)(2,1)}, bf16[128,896]{1,0:T(8,128)(2,1)}, u32[]{:S(2)}, u32[]{:S(2)}) collective-permute-start(bf16[128,896]{1,0:T(8,128)(2,1)} %fusion.21), channel_id=1, source_target_pairs={{0,2},{1,3},{2,0},{3,1},{4,6},{5,7},{6,4},{7,5},{8,10},{9,11},{10,... | collective-permute-start | bytes 688136 | tf_op jit(solution)/shard_map/ppermute | solution.py:574
  6.3 52.5 %collective-permute-start.11 = (s32[2048]{0:T(1024)}, s32[2048]{0:T(1024)S(1)}, u32[]{:S(2)}, u32[]{:S(2)}) collective-permute-start(s32[2048]{0:T(1024)} %param.17), channel_id=1, source_target_pairs={{0,4},{1,5},{2,6},{3,7},{4,0},{5,1},{6,2},{7,3},{8,12},{9,13},{10,... | collective-permute-start | bytes 24584 | tf_op jit(solution)/shard_map/ppermute | solution.py:574
  7.3 51.5 %collective-permute-start = (bf16[512,1024]{1,0:T(8,128)(2,1)}, bf16[512,1024]{1,0:T(8,128)(2,1)S(1)}, u32[]{:S(2)}, u32[]{:S(2)}) collective-permute-start(bf16[512,1024]{1,0:T(8,128)(2,1)} %param.9), channel_id=1, source_target_pairs={{2,4},{3,5},{4,2},{5,3},{10,12},{11,13},{12,10},{13,11},{18,20},{1... | collective-permute-start | bytes 3145736 | tf_op jit(solution)/shard_map/ppermute | solution.py:574
  14.0 49.6 %collective-permute-start.17 = (bf16[128,2304]{1,0:T(8,128)(2,1)}, bf16[128,2304]{1,0:T(8,128)(2,1)}, u32[]{:S(2)}, u32[]{:S(2)}) collective-permute-start(bf16[128,2304]{1,0:T(8,128)(2,1)} %constant_dynamic-update-slice_fusion), channel_id=1, source_target_pairs={{0,2},{1,3},{2,0},{3,1},{4,6},{5,7},{6,4},{7,5},{8,10},{9,11},{10,... | collective-permute-start | bytes 1769480 | tf_op jit(solution)/shard_map/ppermute | solution.py:574
  41.8 20.4 %collective-permute-start.4 = (bf16[128,896]{1,0:T(8,128)(2,1)S(1)}, bf16[128,896]{1,0:T(8,128)(2,1)S(1)}, u32[]{:S(2)}, u32[]{:S(2)}) collective-permute-start(bf16[128,896]{1,0:T(8,128)(2,1)S(1)} %get-tuple-element.142.refs_0_), channel_id=1, source_target_pairs={{0,8},{1,9},{2,10},{3,11},{4,12},{5,13},{6,14},{7,15},{8,0},{9,1},... | collective-permute-start | bytes 688136 | tf_op jit(solution)/shard_map/ppermute | solution.py:574
  42.8 20.6 %collective-permute-start.5 = (bf16[128,896]{1,0:T(8,128)(2,1)S(1)}, bf16[128,896]{1,0:T(8,128)(2,1)S(1)}, u32[]{:S(2)}, u32[]{:S(2)}) collective-permute-start(bf16[128,896]{1,0:T(8,128)(2,1)S(1)} %get-tuple-element.142.refs_0_), channel_id=1, source_target_pairs={{0,16},{1,17},{2,18},{3,19},{4,20},{5,21},{6,22},{7,23},{8,24},{9,... | collective-permute-start | bytes 688136 | tf_op jit(solution)/shard_map/ppermute | solution.py:574
  58.9 28.8 %collective-permute-start.13 = (bf16[512,1024]{1,0:T(8,128)(2,1)S(1)}, bf16[512,1024]{1,0:T(8,128)(2,1)S(1)}, u32[]{:S(2)}, u32[]{:S(2)}) collective-permute-start(bf16[512,1024]{1,0:T(8,128)(2,1)S(1)} %copy-done.17), channel_id=1, source_target_pairs={{2,4},{3,5},{4,2},{5,3},{10,12},{11,13},{12,10},{13,11},{18,20},{1... | collective-permute-start | bytes 3145736 | tf_op jit(solution)/shard_map/ppermute | solution.py:574
  63.7 43.3 %collective-permute-start.1 = (bf16[512,1024]{1,0:T(8,128)(2,1)S(1)}, bf16[512,1024]{1,0:T(8,128)(2,1)S(1)}, u32[]{:S(2)}, u32[]{:S(2)}) collective-permute-start(bf16[512,1024]{1,0:T(8,128)(2,1)S(1)} %broadcast_select_fusion.1.x_ref), channel_id=1, source_target_pairs={{0,1},{1,0},{2,3},{3,2},{4,5},{5,4},{6,7},{7,6},{8,9},{9,8},{10,11... | collective-permute-start | bytes 3145736 | tf_op jit(solution)/shard_map/ppermute | solution.py:574
  92.8 29.6 %collective-permute-start.12 = (bf16[512,1024]{1,0:T(8,128)(2,1)S(1)}, bf16[512,1024]{1,0:T(8,128)(2,1)S(1)}, u32[]{:S(2)}, u32[]{:S(2)}) collective-permute-start(bf16[512,1024]{1,0:T(8,128)(2,1)S(1)} %broadcast_select_fusion.1.x_ref), channel_id=1, source_target_pairs={{0,4},{1,5},{2,6},{3,7},{4,0},{5,1},{6,2},{7,3},{8,12},{9,13},{10,... | collective-permute-start | bytes 3145736 | tf_op jit(solution)/shard_map/ppermute | solution.py:574
  92.8 31.6 %collective-permute-start.14 = (bf16[512,1024]{1,0:T(8,128)(2,1)}, bf16[512,1024]{1,0:T(8,128)(2,1)S(1)}, u32[]{:S(2)}, u32[]{:S(2)}) collective-permute-start(bf16[512,1024]{1,0:T(8,128)(2,1)} %broadcast_select_fusion.refs_0_), channel_id=1, source_target_pairs={{0,1},{1,0},{2,3},{3,2},{4,5},{5,4},{6,7},{7,6},{8,9},{9,8},{10,11... | collective-permute-start | bytes 3145736 | tf_op jit(solution)/shard_map/ppermute | solution.py:574
  94.5 25.5 %collective-permute-start.20 = (bf16[128,2304]{1,0:T(8,128)(2,1)S(1)}, bf16[128,2304]{1,0:T(8,128)(2,1)S(1)}, u32[]{:S(2)}, u32[]{:S(2)}) collective-permute-start(bf16[128,2304]{1,0:T(8,128)(2,1)S(1)} %collective-permute-done.18.refs_1_), channel_id=1, source_target_pairs={{0,16},{1,17},{2,18},{3,19},{4,20},{5,21},{6,22},{7,23},{8,24},{9,... | collective-permute-start | bytes 1769480 | tf_op jit(solution)/shard_map/ppermute | solution.py:574
  106.9 34.5 %collective-permute-start.2 = (bf16[512,1024]{1,0:T(8,128)(2,1)S(1)}, bf16[512,1024]{1,0:T(8,128)(2,1)S(1)}, u32[]{:S(2)}, u32[]{:S(2)}) collective-permute-start(bf16[512,1024]{1,0:T(8,128)(2,1)S(1)} %collective-permute-done.1.x_ref), channel_id=1, source_target_pairs={{0,4},{1,5},{2,6},{3,7},{4,0},{5,1},{6,2},{7,3},{8,12},{9,13},{10,... | collective-permute-start | bytes 3145736 | tf_op jit(solution)/shard_map/ppermute | solution.py:574
  110.8 25.8 %collective-permute-start.22 = (bf16[128,2304]{1,0:T(8,128)(2,1)S(1)}, bf16[128,2304]{1,0:T(8,128)(2,1)S(1)}, u32[]{:S(2)}, u32[]{:S(2)}) collective-permute-start(bf16[128,2304]{1,0:T(8,128)(2,1)S(1)} %collective-permute-done.21.refs_4_), channel_id=1, source_target_pairs={{0,8},{1,9},{2,10},{3,11},{4,12},{5,13},{6,14},{7,15},{8,0},{9,1},... | collective-permute-start | bytes 1769480 | tf_op jit(solution)/shard_map/ppermute | solution.py:574
  122.4 58.2 %collective-permute-start.15 = (bf16[512,1024]{1,0:T(8,128)(2,1)}, bf16[512,1024]{1,0:T(8,128)(2,1)}, u32[]{:S(2)}, u32[]{:S(2)}) collective-permute-start(bf16[512,1024]{1,0:T(8,128)(2,1)} %broadcast_select_fusion.refs_0_), channel_id=1, source_target_pairs={{0,4},{1,5},{2,6},{3,7},{4,0},{5,1},{6,2},{7,3},{8,12},{9,13},{10,... | collective-permute-start | bytes 3145736 | tf_op jit(solution)/shard_map/ppermute | solution.py:574
  124.5 56.2 %collective-permute-start.16 = (bf16[512,1024]{1,0:T(8,128)(2,1)S(1)}, bf16[512,1024]{1,0:T(8,128)(2,1)}, u32[]{:S(2)}, u32[]{:S(2)}) collective-permute-start(bf16[512,1024]{1,0:T(8,128)(2,1)S(1)} %collective-permute-done.14.refs_1_), channel_id=1, source_target_pairs={{0,4},{1,5},{2,6},{3,7},{4,0},{5,1},{6,2},{7,3},{8,12},{9,13},{10,... | collective-permute-start | bytes 3145736 | tf_op jit(solution)/shard_map/ppermute | solution.py:574
  285.2 41.3 %collective-permute-start.42 = (bf16[128,2432]{1,0:T(8,128)(2,1)S(1)}, bf16[128,2432]{1,0:T(8,128)(2,1)S(1)}, u32[]{:S(2)}, u32[]{:S(2)}) collective-permute-start(bf16[128,2432]{1,0:T(8,128)(2,1)S(1)} %copy-done.37), channel_id=1, source_target_pairs={{0,16},{1,17},{2,18},{3,19},{4,20},{5,21},{6,22},{7,23},{8,24},{9,... | collective-permute-start | bytes 1867784 | tf_op jit(solution)/shard_map/ppermute | solution.py:574
  286.5 37.0 %collective-permute-start.45 = (bf16[128,2432]{1,0:T(8,128)(2,1)S(1)}, bf16[128,2432]{1,0:T(8,128)(2,1)S(1)}, u32[]{:S(2)}, u32[]{:S(2)}) collective-permute-start(bf16[128,2432]{1,0:T(8,128)(2,1)S(1)} %copy-done.38), channel_id=1, source_target_pairs={{0,8},{1,9},{2,10},{3,11},{4,12},{5,13},{6,14},{7,15},{8,0},{9,1},... | collective-permute-start | bytes 1867784 | tf_op jit(solution)/shard_map/ppermute | solution.py:574
  286.8 47.6 %collective-permute-start.44 = (bf16[128,2432]{1,0:T(8,128)(2,1)S(1)}, bf16[128,2432]{1,0:T(8,128)(2,1)S(1)}, u32[]{:S(2)}, u32[]{:S(2)}) collective-permute-start(bf16[128,2432]{1,0:T(8,128)(2,1)S(1)} %copy-done.36), channel_id=1, source_target_pairs={{0,8},{1,9},{2,10},{3,11},{4,12},{5,13},{6,14},{7,15},{8,0},{9,1},... | collective-permute-start | bytes 1867784 | tf_op jit(solution)/shard_map/ppermute | solution.py:574
  289.1 31.7 %collective-permute-start.36 = (bf16[128,896]{1,0:T(8,128)(2,1)S(1)}, bf16[128,896]{1,0:T(8,128)(2,1)S(1)}, u32[]{:S(2)}, u32[]{:S(2)}) collective-permute-start(bf16[128,896]{1,0:T(8,128)(2,1)S(1)} %get-tuple-element.95), channel_id=1, source_target_pairs={{0,8},{1,9},{2,10},{3,11},{4,12},{5,13},{6,14},{7,15},{8,0},{9,1},... | collective-permute-start | bytes 688136 | tf_op jit(solution)/shard_map/ppermute | solution.py:574
  304.1 18.1 %collective-permute-start.38 = (bf16[128,896]{1,0:T(8,128)(2,1)S(1)}, bf16[128,896]{1,0:T(8,128)(2,1)S(1)}, u32[]{:S(2)}, u32[]{:S(2)}) collective-permute-start(bf16[128,896]{1,0:T(8,128)(2,1)S(1)} %add_convert_fusion.9), channel_id=1, source_target_pairs={{0,16},{1,17},{2,18},{3,19},{4,20},{5,21},{6,22},{7,23},{8,24},{9,... | collective-permute-start | bytes 688136 | tf_op jit(solution)/shard_map/ppermute | solution.py:574
  327.0 28.6 %collective-permute-start.41 = (bf16[128,2432]{1,0:T(8,128)(2,1)S(1)}, bf16[128,2432]{1,0:T(8,128)(2,1)S(1)}, u32[]{:S(2)}, u32[]{:S(2)}) collective-permute-start(bf16[128,2432]{1,0:T(8,128)(2,1)S(1)} %copy-done.35), channel_id=1, source_target_pairs={{0,16},{1,17},{2,18},{3,19},{4,20},{5,21},{6,22},{7,23},{8,24},{9,... | collective-permute-start | bytes 1867784 | tf_op jit(solution)/shard_map/ppermute | solution.py:574
  331.1 25.3 %collective-permute-start.43 = (bf16[128,2432]{1,0:T(8,128)(2,1)S(1)}, bf16[128,2432]{1,0:T(8,128)(2,1)S(1)}, u32[]{:S(2)}, u32[]{:S(2)}) collective-permute-start(bf16[128,2432]{1,0:T(8,128)(2,1)S(1)} %add_convert_fusion.6), channel_id=1, source_target_pairs={{0,8},{1,9},{2,10},{3,11},{4,12},{5,13},{6,14},{7,15},{8,0},{9,1},... | collective-permute-start | bytes 1867784 | tf_op jit(solution)/shard_map/ppermute | solution.py:574
  343.9 77.2 %collective-permute-start.25 = (bf16[512,1024]{1,0:T(8,128)(2,1)}, bf16[512,1024]{1,0:T(8,128)(2,1)S(1)}, u32[]{:S(2)}, u32[]{:S(2)}) collective-permute-start(bf16[512,1024]{1,0:T(8,128)(2,1)} %get-tuple-element.80), channel_id=1, source_target_pairs={{0,4},{1,5},{2,6},{3,7},{4,0},{5,1},{6,2},{7,3},{8,12},{9,13},{10,... | collective-permute-start | bytes 3145736 | tf_op jit(solution)/shard_map/ppermute | solution.py:574
  355.6 60.5 %collective-permute-start.29 = (bf16[512,1024]{1,0:T(8,128)(2,1)}, bf16[512,1024]{1,0:T(8,128)(2,1)}, u32[]{:S(2)}, u32[]{:S(2)}) collective-permute-start(bf16[512,1024]{1,0:T(8,128)(2,1)} %get-tuple-element.87), channel_id=1, source_target_pairs={{0,4},{1,5},{2,6},{3,7},{4,0},{5,1},{6,2},{7,3},{8,12},{9,13},{10,... | collective-permute-start | bytes 3145736 | tf_op jit(solution)/shard_map/ppermute | solution.py:574
  356.4 59.6 %collective-permute-start.31 = (bf16[512,1024]{1,0:T(8,128)(2,1)}, bf16[512,1024]{1,0:T(8,128)(2,1)}, u32[]{:S(2)}, u32[]{:S(2)}) collective-permute-start(bf16[512,1024]{1,0:T(8,128)(2,1)} %add_convert_fusion), channel_id=1, source_target_pairs={{0,1},{1,0},{2,3},{3,2},{4,5},{5,4},{6,7},{7,6},{8,9},{9,8},{10,11... | collective-permute-start | bytes 3145736 | tf_op jit(solution)/shard_map/ppermute | solution.py:574
  359.1 22.0 %collective-permute-start.51 = (bf16[128,128]{1,0:T(8,128)(2,1)S(1)}, bf16[128,128]{1,0:T(8,128)(2,1)S(1)}, u32[]{:S(2)}, u32[]{:S(2)}) collective-permute-start(bf16[128,128]{1,0:T(8,128)(2,1)S(1)} %add_convert_fusion.14), channel_id=1, source_target_pairs={{0,2},{1,3},{2,0},{3,1},{4,6},{5,7},{6,4},{7,5},{8,10},{9,11},{10,... | collective-permute-start | bytes 98312 | tf_op jit(solution)/shard_map/ppermute | solution.py:574
  364.5 23.0 %collective-permute-start.40 = (bf16[128,896]{1,0:T(8,128)(2,1)}, bf16[128,896]{1,0:T(8,128)(2,1)}, u32[]{:S(2)}, u32[]{:S(2)}) collective-permute-start(bf16[128,896]{1,0:T(8,128)(2,1)} %get-tuple-element.131), channel_id=1, source_target_pairs={{0,2},{1,3},{2,0},{3,1},{4,6},{5,7},{6,4},{7,5},{8,10},{9,11},{10,... | collective-permute-start | bytes 688136 | tf_op jit(solution)/shard_map/ppermute | solution.py:574
  381.1 40.0 %collective-permute-start.27 = (bf16[512,1024]{1,0:T(8,128)(2,1)}, bf16[512,1024]{1,0:T(8,128)(2,1)}, u32[]{:S(2)}, u32[]{:S(2)}) collective-permute-start(bf16[512,1024]{1,0:T(8,128)(2,1)} %add_convert_fusion.1), channel_id=1, source_target_pairs={{0,1},{1,0},{2,3},{3,2},{4,5},{5,4},{6,7},{7,6},{8,9},{9,8},{10,11... | collective-permute-start | bytes 3145736 | tf_op jit(solution)/shard_map/ppermute | solution.py:574
  387.6 21.7 %collective-permute-start.52 = (bf16[128,128]{1,0:T(8,128)(2,1)S(1)}, bf16[128,128]{1,0:T(8,128)(2,1)S(1)}, u32[]{:S(2)}, u32[]{:S(2)}) collective-permute-start(bf16[128,128]{1,0:T(8,128)(2,1)S(1)} %get-tuple-element.143), channel_id=1, source_target_pairs={{0,1},{1,0},{2,3},{3,2},{4,5},{5,4},{6,7},{7,6},{8,9},{9,8},{10,11... | collective-permute-start | bytes 98312 | tf_op jit(solution)/shard_map/ppermute | solution.py:574
  409.3 56.1 %collective-permute-start.48 = (bf16[128,2432]{1,0:T(8,128)(2,1)}, bf16[128,2432]{1,0:T(8,128)(2,1)}, u32[]{:S(2)}, u32[]{:S(2)}) collective-permute-start(bf16[128,2432]{1,0:T(8,128)(2,1)} %get-tuple-element.129), channel_id=1, source_target_pairs={{0,2},{1,3},{2,0},{3,1},{4,6},{5,7},{6,4},{7,5},{8,10},{9,11},{10,... | collective-permute-start | bytes 1867784 | tf_op jit(solution)/shard_map/ppermute | solution.py:574
  418.3 58.6 %collective-permute-start.32 = (bf16[512,1024]{1,0:T(8,128)(2,1)S(1)}, bf16[512,1024]{1,0:T(8,128)(2,1)S(1)}, u32[]{:S(2)}, u32[]{:S(2)}) collective-permute-start(bf16[512,1024]{1,0:T(8,128)(2,1)S(1)} %fusion.13), channel_id=1, source_target_pairs={{2,4},{3,5},{4,2},{5,3},{10,12},{11,13},{12,10},{13,11},{18,20},{1... | collective-permute-start | bytes 3145736 | tf_op jit(solution)/shard_map/ppermute | solution.py:574
  423.1 65.1 %collective-permute-start.28 = (bf16[512,1024]{1,0:T(8,128)(2,1)S(1)}, bf16[512,1024]{1,0:T(8,128)(2,1)S(1)}, u32[]{:S(2)}, u32[]{:S(2)}) collective-permute-start(bf16[512,1024]{1,0:T(8,128)(2,1)S(1)} %fusion.12), channel_id=1, source_target_pairs={{2,4},{3,5},{4,2},{5,3},{10,12},{11,13},{12,10},{13,11},{18,20},{1... | collective-permute-start | bytes 3145736 | tf_op jit(solution)/shard_map/ppermute | solution.py:574
  (60 other events, 1027.8 us)

commit v2 on v1

v2 whole, which is shorter than its diff:
```python
from functools import partial

import jax
import jax.numpy as jnp
from jax import lax
from jax.experimental import pallas as pl
from jax.experimental.pallas import tpu as pltpu
from jax.sharding import Mesh
from jax.sharding import PartitionSpec as P

HD = 64
ROT = 16
L = 2048
LANES = 128
EPSILON = 1e-05
MASKED = -1e30
AXES = ("pair", "core", "half", "m")
PIECES = 4
PIECE = L // PIECES
SEG_LANE = 64
DOCS = 5
LSE_LANE = SEG_LANE + DOCS
DELTA_LANE = 64
MIB = 1024 * 1024
F32 = jnp.float32
BF16 = jnp.bfloat16


def dot_nn(left, right):
    return lax.dot_general(left, right, (((1,), (0,)), ((), ())), preferred_element_type=F32)


def dot_nt(left, right):
    return lax.dot_general(left, right, (((1,), (1,)), ((), ())), preferred_element_type=F32)


def dot_tn(left, right):
    return lax.dot_general(left, right, (((0,), (0,)), ((), ())), preferred_element_type=F32)


def lanes_of(shape):
    return lax.broadcasted_iota(jnp.int32, shape, len(shape) - 1)


def rows_of(shape):
    return lax.broadcasted_iota(jnp.int32, shape, len(shape) - 2)


def normalize(x):
    rows = x.astype(F32)
    centered = rows - jnp.mean(rows, axis=-1, keepdims=True)
    return centered * lax.rsqrt(jnp.mean(centered * centered, axis=-1, keepdims=True) + EPSILON)


def split3(column):
    high = column.astype(BF16).astype(F32)
    rest = column - high
    middle = rest.astype(BF16).astype(F32)
    return high, middle, rest - middle


def with_lanes(base, first, columns):
    lane = lanes_of(base.shape)
    for offset, column in enumerate(columns):
        base = jnp.where(lane == first + offset, column, base)
    return base


def params():
    return pltpu.CompilerParams(vmem_limit_bytes=60 * MIB)


def fenced(kernel, inputs, after):
    return lambda *refs: kernel(*refs[:inputs], *refs[inputs + after :])


ANYWHERE = pl.BlockSpec(memory_space=pl.ANY)


def whole(shape, **kw):
    return pl.BlockSpec(shape, lambda *_: (0,) * len(shape), **kw)


def once(shape):
    return whole(shape, pipeline_mode=pl.Buffered(1))


def cost(flops, nbytes, trans=0):
    return pl.CostEstimate(flops=int(flops), bytes_accessed=int(nbytes), transcendentals=int(trans))


def hops(pairs):
    near = [0] + [1 << b for b in range(pairs.bit_length() - 1)]
    far = sorted((j for j in range(pairs) if j not in near), key=lambda j: (j.bit_count(), j))
    return near, far


def block_places(info_ref, pairs, rows):
    near, far = hops(pairs)
    return pair_places(info_ref, near + far, rows)


def pair_places(info_ref, order, rows):
    core, pair = info_ref[1], info_ref[2]
    for j in order:
        base = (pair ^ j) * 2
        yield pl.multiple_of((base + core) * rows, rows), pl.multiple_of((base + 1 - core) * rows, rows)


def block_refs(refs, pairs):
    near, far = hops(pairs)
    refs = list(refs)
    for _ in near:
        both = refs.pop(0)
        yield both.at[0], both.at[1]
    for _ in far:
        yield refs.pop(0), refs.pop(0)


def block_shapes(pairs, rows, width):
    near, far = hops(pairs)
    return [(2, rows, width)] * len(near) + [(rows, width)] * (2 * len(far))


def assemble_first_kernel(pairs, rows, width, info_ref, *refs):
    weight_ref, gb_ref, small = refs[-3:]
    for offs, both in zip(pair_places(info_ref, range(pairs), rows), refs[:-3]):
        for off, part in zip(offs, (both.at[0], both.at[1])):
            weight_ref[pl.ds(off, rows), :] = part[:, :width]
            small[pl.ds(off, rows), :] = part[:, width:].astype(F32)
    gb_ref[...] = small[...].T[:8, :]


def assemble_first(info, parts, pairs, width):
    rows = parts[0].shape[1]
    feats = pairs * 2 * rows
    return pl.pallas_call(
        partial(assemble_first_kernel, pairs, rows, width),
        out_shape=(jax.ShapeDtypeStruct((feats, width), BF16), jax.ShapeDtypeStruct((8, feats), F32)),
        in_specs=[pl.BlockSpec(memory_space=pltpu.SMEM)] + [pl.BlockSpec(memory_space=pltpu.VMEM)] * len(parts),
        scratch_shapes=[pltpu.VMEM((feats, LANES), F32)],
        compiler_params=params(),
        cost_estimate=cost(0, 4 * feats * width),
        name="assemble_qkv",
    )(info, *parts)


def assemble_second_kernel(pairs, rows, widths, info_ref, *refs):
    outs = refs[-len(widths) :]
    for offs, parts in zip(block_places(info_ref, pairs, rows), block_refs(refs[: -len(widths)], pairs)):
        for off, part in zip(offs, parts):
            start = 0
            for out, width in zip(outs, widths):
                out[pl.ds(off, rows), :] = part[:, start : start + width]
                start += width


def assemble_second(info, parts, pairs, widths):
    rows = parts[0].shape[1]
    feats = pairs * 2 * rows
    return pl.pallas_call(
        partial(assemble_second_kernel, pairs, rows, widths),
        out_shape=tuple(jax.ShapeDtypeStruct((feats, w), BF16) for w in widths),
        in_specs=[pl.BlockSpec(memory_space=pltpu.SMEM)] + [pl.BlockSpec(memory_space=pltpu.VMEM)] * len(parts),
        compiler_params=params(),
        cost_estimate=cost(0, 4 * feats * sum(widths)),
        name="assemble_ffn",
    )(info, *parts)


def turn(values, cosine, sine_up, sine_down):
    return (
        values * cosine
        + pltpu.roll(values, ROT // 2, 1) * sine_up
        + pltpu.roll(values, LANES - ROT // 2, 1) * sine_down
    )


def project_kernel(heads, info_ref, xa_ref, xb_ref, w_ref, gb_ref, turn_ref, feature_ref, *refs):
    n_ref, q_ref, k_ref, v_ref = refs[-4:]
    first_piece = pl.program_id(0) < pl.num_programs(0) // 2
    normalized = normalize(jnp.where(first_piece, xa_ref[...], xb_ref[...]))
    n_ref[0] = normalized
    first = (normalized * gb_ref[0:1, :] + gb_ref[2:3, :]).astype(BF16)
    projected = dot_nn(first, w_ref[...])
    cosine, up, down = (turn_ref[:, n * LANES : (n + 1) * LANES] for n in range(3))
    query_feature, key_feature = (feature_ref[:, n * LANES : (n + 1) * LANES].astype(F32) for n in range(2))
    lane = lanes_of(cosine.shape)
    low = lane < HD
    value_feature = ((lane >= DELTA_LANE) & (lane < DELTA_LANE + 3)).astype(F32)

    def part(offset):
        tile = projected[:, offset // LANES * LANES : offset // LANES * LANES + LANES]
        return pltpu.roll(tile, HD, 1) if offset % LANES else tile

    for h in range(heads):
        sl = slice(h * LANES, (h + 1) * LANES)
        base = h * 3 * HD
        query = turn(part(base), cosine, up, down) * HD ** (-0.5)
        key = turn(part(base + HD), cosine, up, down)
        q_ref[0, :, sl] = jnp.where(low, query, query_feature).astype(BF16)
        k_ref[0, :, sl] = jnp.where(low, key, key_feature).astype(BF16)
        v_ref[0, :, sl] = jnp.where(low, part(base + 2 * HD), value_feature).astype(BF16)


def project(r, info, xa, xb, weight, gb, tables, stacks, after=(), block=256):
    feats, width = weight.shape
    heads = width // (3 * HD)
    steps = PIECE // block
    shapes = [(PIECES, PIECE, feats)] + [(PIECES, PIECE, heads * LANES)] * 3
    kinds = [F32, BF16, BF16, BF16]
    piece = lambda i: r + 2 * (i // steps)
    table = lambda n: pl.BlockSpec((block, n * LANES), lambda i, info: ((info[0] ^ piece(i)) * steps + i % steps, 0))
    inputs = [info, xa, xb, weight, gb, *tables]
    return pl.pallas_call(
        partial(project_kernel, heads),
        grid_spec=pltpu.PrefetchScalarGridSpec(
            num_scalar_prefetch=1,
            grid=(2 * steps,),
            in_specs=[
                pl.BlockSpec((block, feats), lambda i, info: (jnp.minimum(i, steps - 1), 0)),
                pl.BlockSpec((block, feats), lambda i, info: (jnp.maximum(i - steps, 0), 0)),
                once((feats, width)),
                once((8, feats)),
                table(3),
                table(2),
            ]
            + [ANYWHERE] * (len(stacks) + len(after)),
            out_specs=[pl.BlockSpec((1, block, s[2]), lambda i, info: (piece(i), i % steps, 0)) for s in shapes],
        ),
        out_shape=[jax.ShapeDtypeStruct(s, kind) for s, kind in zip(shapes, kinds)],
        input_output_aliases={len(inputs) + n: n for n in range(len(stacks))},
        compiler_params=params(),
        cost_estimate=cost(4 * PIECE * feats * width, 2 * (feats * width + 12 * PIECE * feats)),
        name=f"project_{r}",
    )(*inputs, *stacks, *after)


def attend_kernel(heads, info_ref, q_ref, k_ref, v_ref, o_ref, qb_ref):
    me = info_ref[0]
    causal = lanes_of((PIECE, PIECE)) <= rows_of((PIECE, PIECE))
    low = lanes_of((PIECE, LANES)) < HD
    at = [pl.multiple_of((me ^ p) * PIECE, PIECE) for p in range(PIECES)]
    for i in range(PIECES):
        rows = pl.ds(at[i], PIECE)
        outs = []
        for h in range(heads):
            sl = slice(h * LANES, (h + 1) * LANES)
            query = q_ref[rows, sl]
            scores = [dot_nt(query, k_ref[pl.ds(at[j], PIECE), sl]) for j in range(i + 1)]
            scores[-1] = jnp.where(causal, scores[-1], MASKED)
            top = jnp.max(scores[0], axis=-1, keepdims=True)
            for s in scores[1:]:
                top = jnp.maximum(top, jnp.max(s, axis=-1, keepdims=True))
            out = total = None
            for j, s in enumerate(scores):
                weight = jnp.exp(s - top)
                part = jnp.sum(weight, axis=-1, keepdims=True)
                term = dot_nn(weight.astype(BF16), v_ref[pl.ds(at[j], PIECE), sl])
                total = part if total is None else total + part
                out = term if out is None else out + term
            outs.append(out * (1.0 / total))
            log_total = split3(top + jnp.log(total))
            qb_ref[rows, sl] = with_lanes(query.astype(F32), LSE_LANE, [-c for c in log_total]).astype(BF16)
        for h in range(0, heads, 2):
            o_ref[rows, h * HD : h * HD + LANES] = jnp.where(low, outs[h], pltpu.roll(outs[h + 1], HD, 1))


def attend(info, queries, keys, values, group, heads, after=()):
    full = queries.shape[2]
    width = heads * LANES
    own = pl.BlockSpec((L, width), lambda i, info: (0, group))
    return pl.pallas_call(
        fenced(partial(attend_kernel, heads), 4, len(after)),
        grid_spec=pltpu.PrefetchScalarGridSpec(
            num_scalar_prefetch=1,
            grid=(1,),
            in_specs=[own] * 3 + [ANYWHERE] * len(after),
            out_specs=[whole((L, heads * HD)), whole((L, width))],
        ),
        out_shape=[jax.ShapeDtypeStruct((L, heads * HD), F32), jax.ShapeDtypeStruct((L, width), BF16)],
        compiler_params=params(),
        cost_estimate=cost(heads * L * L * LANES * 4, 5 * L * width, heads * L * L // 2),
        name=f"attention_forward_{group}",
    )(info, *(a.reshape(L, full) for a in (queries, keys, values)), *after)


def gelu_parts(h):
    bell = jnp.exp2(h * h * (-0.5 * 1.4426950408889634))
    t = pl.reciprocal(1.0 + (0.3275911 * 0.5**0.5) * jnp.abs(h))
    poly = t * (
        0.127414796 + t * (-0.142248368 + t * (0.7107068705 + t * (-0.7265760135 + t * 0.5307027145)))
    )
    tail = poly * bell
    return jnp.where(h < 0, tail, 1.0 - tail), bell * 0.3989422804014327


def norm_columns(sums_ref):
    wide = jnp.concatenate([sums_ref[...], jnp.zeros((LANES - 8, sums_ref.shape[1]), F32)], axis=0)
    return wide.T


def write_parts(info_ref, total, small, refs):
    width, rows = total.shape[1], refs[0].shape[1]
    for offs, both in zip(pair_places(info_ref, range(len(refs)), rows), refs):
        for n, off in enumerate(offs):
            both[n, :, :width] = total[pl.ds(off, rows), :].astype(BF16)
            both[n, :, width:] = small[pl.ds(off, rows), :].astype(BF16)


def feed_kernel(groups, parts, n_ref, *refs):
    o_refs, refs = refs[:groups], refs[groups:]
    wd_ref, we_ref, ws_ref, gb_ref, br01_ref, br23_ref, activated_ref, slope_ref, b_now = refs
    step = pl.program_id(0)
    rows = PIECE // parts
    for n in range(parts):
        sl = slice(n * rows, (n + 1) * rows)
        second = (n_ref[sl, :] * gb_ref[1:2, :] + gb_ref[3:4, :]).astype(BF16)
        hidden = dot_nn(second, we_ref[...])
        cdf, density = gelu_parts(hidden)
        activated = (hidden * cdf).astype(BF16)
        activated_ref[sl, :] = activated
        slope_ref[sl, :] = cdf + hidden * density
        attended = jnp.concatenate([o[sl, :] for o in o_refs], axis=1).astype(BF16)
        b_now[sl, :] = (dot_nt(attended, wd_ref[...]) + dot_nt(activated, ws_ref[...])).astype(BF16)

    @pl.when(step < 2)
    def _():
        br01_ref[0] = b_now[...]

    @pl.when(step >= 2)
    def _():
        br23_ref[0] = b_now[...]


def feed(normalized, outs, wd, we, ws, gb, after=(), parts=2):
    feats, hidden = we.shape
    two = (2, PIECE, feats)
    by_step = lambda i: (i, 0)
    inputs = [normalized.reshape(L, feats), *outs, wd, we, ws, gb]
    return pl.pallas_call(
        fenced(partial(feed_kernel, len(outs), parts), len(inputs), len(after)),
        grid=(PIECES,),
        in_specs=[pl.BlockSpec((PIECE, feats), by_step)]
        + [pl.BlockSpec((PIECE, o.shape[1]), by_step) for o in outs]
        + [once(w.shape) for w in (wd, we, ws, gb)]
        + [ANYWHERE] * len(after),
        out_specs=[
            pl.BlockSpec((1, PIECE, feats), lambda i: (jnp.minimum(i, 1), 0, 0)),
            pl.BlockSpec((1, PIECE, feats), lambda i: (jnp.maximum(i - 2, 0), 0, 0)),
            pl.BlockSpec((PIECE, hidden), by_step),
            pl.BlockSpec((PIECE, hidden), by_step),
        ],
        out_shape=[jax.ShapeDtypeStruct(two, BF16)] * 2
        + [jax.ShapeDtypeStruct((L, hidden), BF16), jax.ShapeDtypeStruct((L, hidden), F32)],
        scratch_shapes=[pltpu.VMEM((PIECE, feats), BF16)],
        compiler_params=params(),
        cost_estimate=cost(4 * L * feats * hidden, 16 * L * feats),
        name="feed_forward",
    )(*inputs, *after)


def feed_back_kernel(heads, group, n_ref, activated_ref, slope_ref, *refs):
    groups = heads // group
    g_refs, refs = refs[:PIECES], refs[PIECES:]
    o_refs, refs = refs[:groups], refs[groups:]
    (wd_ref, we_ref, ws_ref, gb_ref, sg_ref), refs = refs[:5], refs[5:]
    doa_refs, refs = refs[:groups], refs[groups:]
    grads_ref, g_now, gd, ge, gs, sums = refs
    step, last = pl.program_id(0), pl.num_programs(0) - 1

    @pl.when(step == 0)
    def _():
        for total in (gd, ge, gs, sums):
            total[...] = jnp.zeros_like(total)

    for r in range(PIECES):

        @pl.when(step == r)
        def _():
            g_now[...] = g_refs[r][...]

    g = g_now[...]
    hidden_grad = (dot_nn(g, ws_ref[...]) * slope_ref[...]).astype(BF16)
    normalized = n_ref[...]
    second = (normalized * gb_ref[1:2, :] + gb_ref[3:4, :]).astype(BF16)
    out = jnp.concatenate([o[...] for o in o_refs], axis=1)
    gs[...] += dot_tn(g, activated_ref[...])
    gd[...] += dot_tn(g, out.astype(BF16))
    ge[...] += dot_tn(second, hidden_grad)
    second_grad = dot_nt(hidden_grad, we_ref[...])
    sg_ref[...] = second_grad * gb_ref[1:2, :]
    sums[0:1, :] += jnp.sum(second_grad * normalized, axis=0, keepdims=True)
    sums[1:2, :] += jnp.sum(second_grad, axis=0, keepdims=True)
    attended_grad = dot_nn(g, wd_ref[...]).astype(BF16).astype(F32)
    product = attended_grad * out
    lane = lanes_of((PIECE, LANES))
    for h in range(heads):
        tile = slice(h // 2 * LANES, (h // 2 + 1) * LANES)
        mine = (lane < HD) if h % 2 == 0 else (lane >= HD)
        delta = split3(jnp.sum(jnp.where(mine, product[:, tile], 0.0), axis=-1, keepdims=True))
        grad = attended_grad[:, tile]
        if h % 2:
            grad = pltpu.roll(grad, HD, 1)
        grad = jnp.where(lane < HD, grad, 0.0)
        start = h % group * LANES
        doa_refs[h // group][:, start : start + LANES] = with_lanes(grad, DELTA_LANE, [-c for c in delta]).astype(BF16)

    @pl.when(step == last)
    def _():
        start = 0
        for total in (gd, ge, gs):
            grads_ref[:, start : start + total.shape[1]] = total[...].astype(BF16)
            start += total.shape[1]
        grads_ref[:, start:] = norm_columns(sums).astype(BF16)


def feed_back(normalized, activated, slope, g_parts, outs, wd, we, ws, gb, after=()):
    feats, hidden = we.shape
    heads = wd.shape[1] // HD
    group = heads // len(outs)
    width = wd.shape[1] + 2 * hidden + LANES
    by_step = lambda i: (i, 0)
    step = lambda w: pl.BlockSpec((PIECE, w), by_step)
    inputs = [normalized.reshape(L, feats), activated, slope, *g_parts, *outs, wd, we, ws, gb]
    return pl.pallas_call(
        fenced(partial(feed_back_kernel, heads, group), len(inputs), len(after)),
        grid=(PIECES,),
        in_specs=[step(feats), step(hidden), step(hidden)]
        + [once((PIECE, feats))] * PIECES
        + [step(group * HD)] * len(outs)
        + [once(w.shape) for w in (wd, we, ws, gb)]
        + [ANYWHERE] * len(after),
        out_specs=[step(feats)] + [step(group * LANES)] * len(outs) + [once((feats, width))],
        out_shape=[jax.ShapeDtypeStruct((L, feats), F32)]
        + [jax.ShapeDtypeStruct((L, group * LANES), BF16)] * len(outs)
        + [jax.ShapeDtypeStruct((feats, width), BF16)],
        scratch_shapes=[
            pltpu.VMEM((PIECE, feats), BF16),
            pltpu.VMEM(wd.shape, F32),
            pltpu.VMEM(we.shape, F32),
            pltpu.VMEM(ws.shape, F32),
            pltpu.VMEM((8, feats), F32),
        ],
        compiler_params=params(),
        cost_estimate=cost(8 * L * feats * hidden, 20 * L * feats),
        name="feed_back",
    )(*inputs, *after)


def block_back(query, grad, key, value, causal):
    scores = dot_nt(key, query)
    if causal is not None:
        scores = jnp.where(causal, scores, MASKED)
    probs = jnp.exp(scores)
    score_grad = (probs * dot_nt(value, grad)).astype(BF16)
    return dot_tn(score_grad, key), dot_nn(score_grad, query), dot_nn(probs.astype(BF16), grad)


def triangle_back(load, base, sums, h, causal):
    q0, g0, k0, v0 = load(base)
    q1, g1, k1, v1 = load(base + 1)
    low = block_back(q0, g0, k0, v0, causal)
    side = block_back(q1, g1, k0, v0, None)
    high = block_back(q1, g1, k1, v1, causal)
    dq, dk, dv = sums
    dq[h, base] += low[0]
    dq[h, base + 1] += side[0] + high[0]
    for d, n in ((dk, 1), (dv, 2)):
        d[h, base] += low[n] + side[n]
        d[h, base + 1] += high[n]


def finish_back(pg_ref, tables_ref, table_row, sums, base, near, heads):
    low = lanes_of((PIECE, LANES)) < HD
    dq, dk, dv = sums
    for n in range(2):
        rows = pl.ds(pl.multiple_of(table_row + n * PIECE, PIECE), PIECE)
        cosine = tables_ref[rows, :LANES]
        up, down = -tables_ref[rows, LANES : 2 * LANES], -tables_ref[rows, 2 * LANES :]
        for h in range(0, heads, 2):
            start = h // 2 * 3 * LANES
            q0, q1 = (turn(dq[h + x, base + n] * HD ** (-0.5), cosine, up, down) for x in (0, 1))
            k0, k1 = (turn(dk[h + x, base + n], cosine, up, down) for x in (0, 1))
            v0, v1 = dv[h, base + n], dv[h + 1, base + n]
            for tile, (left, right) in enumerate(((q0, k0), (v0, q1), (k1, v1))):
                pg_ref[near ^ n, :, start + tile * LANES : start + (tile + 1) * LANES] = jnp.where(
                    low, left, pltpu.roll(right, HD, 1)
                ).astype(BF16)


def attend_back_first_kernel(info_ref, q_ref, do_ref, k_ref, v_ref, tables_ref, pg_ref, *refs):
    rests, sums = refs[:3], refs[3:]
    dq, dk, dv = sums
    me, half = info_ref[0], info_ref[3]
    heads = q_ref.shape[1] // LANES
    causal = rows_of((PIECE, PIECE)) <= lanes_of((PIECE, PIECE))
    swapped, native = 2 * (1 - half), 2 * half
    zero = jnp.zeros((PIECE, LANES), F32)
    for h in range(heads):
        sl = slice(h * LANES, (h + 1) * LANES)

        def load(piece):
            rows = pl.ds(pl.multiple_of((me ^ piece) * PIECE, PIECE), PIECE)
            return q_ref[rows, sl], do_ref[rows, sl], k_ref[rows, sl], v_ref[rows, sl]

        pieces = [load(p) for p in range(PIECES)]
        terms = {
            (i, j): block_back(*pieces[i][:2], *pieces[j][2:], None) for j in (0, 1) for i in (2, 3)
        }
        for p in (0, 1):
            dq[h, p] = zero
            dq[h, p + 2] = terms[p + 2, 0][0] + terms[p + 2, 1][0]
            for d, n in ((dk, 1), (dv, 2)):
                d[h, p] = terms[2, p][n] + terms[3, p][n]
                d[h, p + 2] = zero
        triangle_back(load, swapped, sums, h, causal)
        for rest, d in zip(rests, sums):
            for n in range(2):
                rest[h, n] = d[h, native + n]
    finish_back(pg_ref, tables_ref, swapped * PIECE, sums, swapped, me % 2, heads)


def attend_back_second_kernel(info_ref, q_ref, do_ref, k_ref, v_ref, tables_ref, *refs):
    rests, pg_ref, sums = refs[:3], refs[3], refs[4:]
    near = info_ref[0] % 2
    heads = q_ref.shape[1] // LANES
    causal = rows_of((PIECE, PIECE)) <= lanes_of((PIECE, PIECE))
    for h in range(heads):
        sl = slice(h * LANES, (h + 1) * LANES)

        def load(piece):
            rows = pl.ds(pl.multiple_of((near ^ piece) * PIECE, PIECE), PIECE)
            return q_ref[rows, sl], do_ref[rows, sl], k_ref[rows, sl], v_ref[rows, sl]

        for rest, d in zip(rests, sums):
            for n in range(2):
                d[h, n] = rest[h, n]
        triangle_back(load, 0, sums, h, causal)
    finish_back(pg_ref, tables_ref, 0, sums, 0, near, heads)


def attend_back(info, queries, grads, keys, values, tables, group, rests=(), after=()):
    width, full = queries.shape[1], keys.shape[2]
    heads = width // LANES
    rest = (heads, 2, PIECE, LANES)
    pg = (2, PIECE, heads * 3 * HD)
    first = not rests
    rows = L if first else L // 2
    place = (lambda info: 0) if first else (lambda info: info[1] ^ info[3])
    own = pl.BlockSpec((rows, width), lambda s, info: (place(info), 0))
    shared = pl.BlockSpec((rows, width), lambda s, info: (place(info), group))
    table = pl.BlockSpec((rows, 3 * LANES), lambda s, info: (0 if first else info[3], 0))
    inputs = [info, queries, grads, keys.reshape(L, full), values.reshape(L, full), tables, *rests]
    blocks = 7 if first else 3
    return pl.pallas_call(
        fenced(attend_back_first_kernel if first else attend_back_second_kernel, len(inputs), len(after)),
        grid_spec=pltpu.PrefetchScalarGridSpec(
            num_scalar_prefetch=1,
            grid=(1,),
            in_specs=[own, own, shared, shared, table] + [whole(rest)] * len(rests) + [ANYWHERE] * len(after),
            out_specs=[whole(pg)] + [whole(rest)] * (3 if first else 0),
            scratch_shapes=[pltpu.VMEM((heads, PIECES if first else 2, PIECE, LANES), F32)] * 3,
        ),
        out_shape=[jax.ShapeDtypeStruct(pg, BF16)] + [jax.ShapeDtypeStruct(rest, F32)] * (3 if first else 0),
        compiler_params=params(),
        cost_estimate=cost(blocks * heads * PIECE * PIECE * LANES * 10, 12 * L * width, blocks * heads * PIECE * PIECE),
        name=f"attention_backward_{group}" + ("a" if first else "b"),
    )(*inputs, *after)


def project_back_kernel(pairs, groups, final, info_ref, *refs):
    pg_refs, refs = refs[:groups], refs[groups:]
    (n_ref, sg_ref, w_ref, gb_ref), refs = refs[:4], refs[4:]
    if final:
        (gq_in, sums_in, e_ref), refs = refs[:3], refs[3:]
        *part_refs, gq, sums, small = refs
    else:
        e_ref, gq, sums = refs
    step, last = pl.program_id(0), pl.num_programs(0) - 1

    @pl.when(step == 0)
    def _():
        gq[...] = gq_in[...] if final else jnp.zeros_like(gq)
        sums[...] = sums_in[...] if final else jnp.zeros_like(sums)

    normalized = n_ref[0]
    first = (normalized * gb_ref[0:1, :] + gb_ref[2:3, :]).astype(BF16)
    grad = jnp.concatenate([pg[0] for pg in pg_refs], axis=1)
    first_grad = dot_nt(grad, w_ref[...])
    gq[...] += dot_tn(first, grad)
    e_ref[0] = (first_grad * gb_ref[0:1, :] + sg_ref[0]).astype(BF16)
    sums[0:1, :] += jnp.sum(first_grad * normalized, axis=0, keepdims=True)
    sums[1:2, :] += jnp.sum(first_grad, axis=0, keepdims=True)
    if final:

        @pl.when(step == last)
        def _():
            small[...] = norm_columns(sums)
            write_parts(info_ref, gq, small, part_refs)


def project_back(info, pgs, normalized, sg, weight, gb, pairs, so_far=(), after=()):
    feats, width = weight.shape
    final = bool(so_far)
    swapped = 0 if final else 1
    sums = (8, feats)
    shapes = [(2, feats // (2 * pairs), width + LANES)] * pairs if final else []
    two = (2, PIECE, feats)
    by_step = lambda i, info: (i, 0, 0)
    relative = pl.BlockSpec((1, PIECE, feats), lambda i, info: (2 * (info[1] ^ info[3] ^ swapped) + i, 0, 0))
    inputs = [info, *pgs, normalized, sg.reshape(PIECES, PIECE, feats), weight, gb, *so_far]
    totals = [pltpu.VMEM(weight.shape, F32), pltpu.VMEM(sums, F32)]
    results = [(two, BF16)] + ([(s, BF16) for s in shapes] if final else [(weight.shape, F32), (sums, F32)])
    return pl.pallas_call(
        fenced(partial(project_back_kernel, pairs, len(pgs), final), len(inputs), len(after)),
        grid_spec=pltpu.PrefetchScalarGridSpec(
            num_scalar_prefetch=1,
            grid=(2,),
            in_specs=[pl.BlockSpec((1, PIECE, pg.shape[2]), by_step) for pg in pgs]
            + [relative, relative]
            + [once(a.shape) for a in (weight, gb, *so_far)]
            + [ANYWHERE] * len(after),
            out_specs=[pl.BlockSpec((1, PIECE, feats), by_step)] + [once(s) for s, _ in results[1:]],
            scratch_shapes=totals + [pltpu.VMEM((feats, LANES), F32)] if final else [],
        ),
        out_shape=[jax.ShapeDtypeStruct(s, kind) for s, kind in results],
        compiler_params=params(),
        cost_estimate=cost(2 * L * feats * width, 6 * L * feats),
        name="project_back_" + ("b" if final else "a"),
    )(*inputs, *after)


def build_tables(segments):
    places = jnp.arange(L, dtype=jnp.int32)
    starts = jnp.zeros_like(segments)
    for value in range(DOCS):
        starts = starts + jnp.where(segments > value, jnp.sum((segments == value).astype(jnp.int32)), 0)
    position = (places - starts).astype(F32)
    lane = jnp.arange(LANES, dtype=jnp.int32)
    inner = lane % HD
    half = ROT // 2
    frequency = 10000.0 ** (-((inner % half).astype(F32) * 2.0 / ROT))
    angles = position[:, None] * frequency[None, :]
    turned = (inner < ROT)[None, :]
    sine = jnp.sin(angles)
    cosine = jnp.where(turned, jnp.cos(angles), 1.0)
    up = jnp.where(turned & (inner >= half)[None, :], sine, 0.0)
    down = jnp.where((inner < half)[None, :], -sine, 0.0)
    feature = lane - SEG_LANE
    is_doc = ((feature >= 0) & (feature < DOCS))[None, :]
    same = segments[:, None] == feature[None, :]
    one = ((lane >= LSE_LANE) & (lane < LSE_LANE + 3))[None, :]
    query_feature = jnp.where(is_doc & ~same, MASKED, 0.0)
    key_feature = jnp.where((is_doc & same) | one, 1.0, 0.0)
    features = jnp.concatenate([query_feature, key_feature], axis=1).astype(BF16)
    return jnp.concatenate([cosine, up, down], axis=1), features


class Wires:
    def __init__(self, mesh):
        self.pairs = mesh.shape["pair"]
        self.sizes = [mesh.shape[a] for a in AXES]

    def send(self, array, target):
        _, cores, halves, ms = self.sizes

        def index(k, c, h, m):
            return ((k * cores + c) * halves + h) * ms + m

        moves = []
        for k in range(self.pairs):
            for c in range(cores):
                for h in range(halves):
                    for m in range(ms):
                        there = target(k, c, h, m)
                        if there is not None:
                            moves.append((index(k, c, h, m), index(*there)))
        return lax.ppermute(array, AXES, moves)

    def core(self, array):
        return self.send(array, lambda k, c, h, m: (k, 1 - c, h, m))

    def near(self, array, native):
        return self.send(array, lambda k, c, h, m: (k, c, h, 1 - m) if (c == h) == native else None)

    def core_from(self, array, native):
        return self.send(array, lambda k, c, h, m: (k, 1 - c, h, m) if (c == h) == native else None)

    def near_all(self, array):
        return self.send(array, lambda k, c, h, m: (k, c, h, 1 - m))

    def across(self, array):
        return self.send(array, lambda k, c, h, m: (k, c, 1 - h, 1 - m))

    def half(self, array):
        return self.send(array, lambda k, c, h, m: (k, c, 1 - h, m))

    def regroup(self, array):
        return self.send(array, lambda k, c, h, m: (k, 1 - c, 1 - h, m) if c != h else None)

    def plane(self, array, bit):
        return self.send(array, lambda k, c, h, m: (k ^ bit, c, h, m))

    def gather_near(self, both):
        return [both] + [self.plane(both, j) for j in hops(self.pairs)[0][1:]]

    def gather_far(self, parts):
        near, far = hops(self.pairs)
        a_parts = {j: part[0] for j, part in zip(near, parts)}
        b_parts = {j: part[1] for j, part in zip(near, parts)}
        result = list(parts)
        for j in far:
            low, high = j & -j, 1 << (j.bit_length() - 1)
            a_parts[j] = self.plane(a_parts[j ^ low], low)
            b_parts[j] = self.plane(b_parts[j ^ high], high)
            result += [a_parts[j], b_parts[j]]
        return result

    def gather_direct(self, both):
        return [both] + [self.plane(both, j) for j in range(1, self.pairs)]

    def scatter_direct(self, parts):
        return [self.plane(part, j) for j, part in enumerate(parts) if j]


def on_device(mesh, inputs, qkv_weight, dense_weight, expand_weight, shrink_weight, norm_gains, norm_biases, cotangent, segments):
    wires = Wires(mesh)
    pairs = wires.pairs
    pair, core, half, near = (lax.axis_index(a) for a in AXES)
    native = core == half
    me = 2 * core + near
    info = jnp.stack([me, core, pair, half]).astype(jnp.int32)

    def since(value, *done):
        return lax.optimization_barrier((value, done))[0]

    def at(values):
        return lax.optimization_barrier(values)

    def swap_weights(block, swapped):
        own = jnp.where(native, block, swapped)
        return jnp.stack([own, wires.core(jnp.where(native, swapped, block))])

    def swap_grads(both):
        other = wires.core(both[1])
        small = (both[0][:, -LANES:].astype(F32) + other[:, -LANES:].astype(F32)).astype(BF16)
        mine, sent = jnp.where(native, both[0], other), jnp.where(native, other, both[0])
        return [jnp.concatenate([a[:, :-LANES], small], axis=1) for a in (mine, sent)]

    def core_sum(parts):
        return parts[0].astype(F32) + wires.core(parts[1]).astype(F32)

    def since(value, *done):
        return lax.optimization_barrier((value, done))[0]

    def since(value, *done):
        return lax.optimization_barrier((value, done))[0]

    small = jnp.concatenate([norm_gains, norm_biases], axis=0).T
    first_block = jnp.concatenate([qkv_weight, jnp.pad(small, ((0, 0), (0, LANES - 4)))], axis=1)
    first_swapped = wires.half(first_block)
    other_segments = wires.core(since(segments, first_block))
    x_swapped = wires.regroup(since(inputs, other_segments))
    x_near = wires.near(since(inputs, other_segments), True)
    first_both = swap_weights(first_block, first_swapped)
    first_parts = wires.gather_direct(first_both)
    tables = build_tables(jnp.where(native, since(segments, first_both), other_segments))
    first_parts = since(first_parts, tables)
    qkv_full, gb = assemble_first(info, first_parts, pairs, qkv_weight.shape[1])
    x_swapped, x_near, qkv_full, gb = at((x_swapped, x_near, qkv_full, gb))
    x_mine = jnp.where(native, inputs, x_swapped)
    x_far = wires.near(x_swapped, False)
    x_core = wires.core(x_mine)
    stacks = project(0, info, x_mine, x_core, qkv_full, gb, tables, ())

    stacks, x_near, x_far = at((stacks, x_near, x_far))
    second_a = jnp.concatenate([dense_weight, expand_weight], axis=1)
    x_beside = jnp.where(native, x_near, x_far)
    x_last = wires.core(x_beside)
    a_swapped = wires.half(since(second_a, x_beside))
    stacks = project(1, info, x_beside, x_last, qkv_full, gb, tables, stacks)
    stacks, a_swapped = at((stacks, a_swapped))
    normalized, queries, keys, values = stacks

    b_swapped = wires.half(since(shrink_weight, a_swapped))
    a_both = swap_weights(second_a, a_swapped)
    a_near = wires.gather_near(a_both)
    out_0, queries_0 = attend(info, queries, keys, values, 0, 2, after=(a_both,))
    out_0, a_near, b_swapped = at((out_0, a_near, b_swapped))
    b_both = swap_weights(shrink_weight, b_swapped)
    a_parts = wires.gather_far(a_near)
    b_near = wires.gather_near(b_both)
    g_swapped = wires.regroup(since(cotangent, b_swapped))
    g_near = wires.near(since(cotangent, b_swapped), True)
    out_1, queries_1 = attend(info, queries, keys, values, 1, 2, after=(out_0, b_both))
    out_1, a_parts, b_near = at((out_1, a_parts, b_near))
    b_parts = wires.gather_far(b_near)
    widths = (dense_weight.shape[1], expand_weight.shape[1], shrink_weight.shape[1])
    dense_full, expand_full = assemble_second(info, a_parts, pairs, widths[:2])
    dense_full, expand_full, b_parts = at((dense_full, expand_full, b_parts))
    (shrink_full,) = assemble_second(info, b_parts, pairs, widths[2:])
    shrink_full, g_swapped, g_near = at((shrink_full, g_swapped, g_near))
    g_far = wires.near(g_swapped, False)
    g_mine = jnp.where(native, cotangent, g_swapped)
    g_core = wires.core(g_mine)
    results = feed(normalized, (out_0, out_1), dense_full, expand_full, shrink_full, gb, after=(g_mine,))
    results, g_near, g_far, g_core = at((results, g_near, g_far, g_core))
    *branches, activated, slope = results
    g_beside = jnp.where(native, g_near, g_far)
    g_parts = [g_mine, g_beside, g_core, wires.core(g_beside)]

    branch = core_sum(branches)
    passed = branch[1].astype(BF16)
    branch_far = wires.near(passed, False)
    branch_near = wires.near(passed, True)
    results = feed_back(
        normalized, activated, slope, g_parts, (out_0, out_1), dense_full, expand_full, shrink_full, gb, after=(passed,)
    )
    results, branch_far, branch_near = at((results, branch_far, branch_near))
    second_e, *grads, feed_grads = results

    turns = tables[0]
    feed_both = lax.psum_scatter(feed_grads, "pair", scatter_dimension=0, tiled=True)
    branch_sent = (branch[0] + branch_far.astype(F32)).astype(BF16)
    branch_back = wires.regroup(branch_sent)
    pg_0, *rests_0 = attend_back(info, queries_0, grads[0], keys, values, turns, 0, after=(branch_sent,))
    pg_0, rests_0, branch_back = at((pg_0, rests_0, branch_back))
    pg_1, *rests_1 = attend_back(info, queries_1, grads[1], keys, values, turns, 1, after=(pg_0,))
    results = project_back(info, (pg_0, pg_1), normalized, second_e, qkv_full, gb, pairs)
    results = at(results)
    e_swapped, *so_far = results

    e_core = wires.core_from(e_swapped, True)
    e_swapped = e_swapped.astype(F32) + e_core.astype(F32)
    e_passed = e_swapped[1].astype(BF16)
    e_far = wires.near(e_passed, False)
    (pg_0,) = attend_back(info, queries_0, grads[0], keys, values, turns, 0, rests_0, after=(e_passed, *so_far))
    pg_0, e_far = at((pg_0, e_far))
    e_sent = (e_swapped[0] + e_far.astype(F32)).astype(BF16)
    e_back = wires.regroup(e_sent)
    (pg_1,) = attend_back(info, queries_1, grads[1], keys, values, turns, 1, rests_1, after=(pg_0, e_sent))
    pg_1, feed_both = at((pg_1, feed_both))
    feed_both = feed_both.reshape(2, qkv_weight.shape[0], -1)
    feed_both = jnp.where(core == 0, feed_both, feed_both[::-1])
    feed_mine, feed_sent = swap_grads(feed_both)
    feed_arrived = wires.half(feed_sent)
    results = project_back(
        info, (pg_0, pg_1), normalized, second_e, qkv_full, gb, pairs, so_far, after=(feed_sent,)
    )
    results, e_back = at((results, e_back))
    e_native, *qkv_grads = results
    e_core = wires.core_from(e_native, False)
    qkv_near = wires.scatter_direct(qkv_grads)
    e_sum = e_native.astype(F32) + e_core.astype(F32)
    e_passed = e_sum[1].astype(BF16)
    e_near = wires.near(e_passed, True)
    qkv_near, feed_arrived = since((qkv_near, feed_arrived), e_passed)
    rows_f32 = inputs.astype(F32)
    layer_out = jnp.where(native, branch[0] + branch_near.astype(F32), branch_back.astype(F32))
    layer_out = (rows_f32 + layer_out).astype(BF16)
    feed_total = feed_mine.astype(F32) + feed_arrived.astype(F32)
    qkv_both = sum(part.astype(F32) for part in (qkv_grads[0], *qkv_near)).astype(BF16)
    qkv_mine, qkv_sent = swap_grads(qkv_both)
    smalls = jnp.concatenate([qkv_mine[:, -LANES:], feed_mine[:, -LANES:]], axis=1)
    smalls = since(smalls, e_near)
    qkv_total = qkv_mine.astype(F32) + wires.half(since(qkv_sent, e_near)).astype(F32)
    arrived = wires.near_all(smalls).astype(F32) + wires.across(smalls).astype(F32)
    attention_norm_grad = (qkv_total[:, -LANES:] + arrived[:, :LANES])[:, :8].T[:2]
    feedforward_norm_grad = (feed_total[:, -LANES:] + arrived[:, LANES:])[:, :8].T[:2]
    e = jnp.where(native, e_sum[0] + e_near.astype(F32), e_back.astype(F32))

    centered = rows_f32 - jnp.mean(rows_f32, axis=-1, keepdims=True)
    inv_scale = lax.rsqrt(jnp.mean(centered * centered, axis=-1, keepdims=True) + EPSILON)
    normalized = centered * inv_scale
    input_grad = cotangent.astype(F32) + inv_scale * (
        e - jnp.mean(e, axis=-1, keepdims=True) - normalized * jnp.mean(e * normalized, axis=-1, keepdims=True)
    )
    return (
        layer_out,
        input_grad,
        qkv_total[:, :-LANES],
        feed_total[:, : widths[0]],
        feed_total[:, widths[0] : widths[0] + widths[1]],
        feed_total[:, widths[0] + widths[1] : -LANES],
        attention_norm_grad,
        feedforward_norm_grad,
    )


def solution(mesh):
    dp, tensor = mesh.shape["dp"], mesh.shape["tensor"]
    fine = Mesh(mesh.devices.reshape(dp // 2, 2, 2, tensor // 2), AXES)
    data, split = ("pair", "core"), ("half", "m")
    tokens, weight, norm = P(AXES, None), P(data, split), P(None, data)
    return jax.shard_map(
        partial(on_device, fine),
        mesh=fine,
        in_specs=(tokens, weight, weight, weight, weight, norm, norm, tokens, P(data)),
        out_specs=(tokens, tokens, weight, weight, weight, weight, norm, norm),
        check_vma=False,
    )
```

time: 499 us -> 430 us (0.86)
  the two profiles are of different devices: /device:TPU:1 before, /device:TPU:0 now
where the time goes in v2:
time: 430 us; the launch traced here: 422 us
  Pallas kernels  182 us (42%)
  starting transfers between devices  94.1 us (22%)
  waiting for transfers between devices  70.9 us (16%)
  other arithmetic  40.6 us (9%)
  local copies, waits for them, and re-layouts  19.2 us (4%)
  between operations  15.1 us (4%)
    ppermute x46, starting transfers between devices, send(): return lax.ppermute(array, AXES, moves)  94.1 us
    ppermute x46, waiting for transfers between devices, send(): return lax.ppermute(array, AXES, moves)  70.9 us
    pallas_call x4, Pallas kernels, attend_back(): pl.pallas_call(fenced(attend_back_first_kernel if first else attend_back_...  52.6 us
    pallas_call x1, Pallas kernels, feed_back(): pl.pallas_call(fenced(partial(feed_back_kernel, heads, group), len(inputs...  33.6 us
    pallas_call x2, Pallas kernels, attend(): pl.pallas_call(fenced(partial(attend_kernel, heads), 4, len(after)), grid...  24.5 us
    pallas_call x2, Pallas kernels, project_back(): pl.pallas_call(fenced(partial(project_back_kernel, pairs, len(pgs), final...  21.8 us
    pallas_call x1, Pallas kernels, feed(): pl.pallas_call(fenced(partial(feed_kernel, len(outs), parts), len(inputs)...  21.6 us
    pallas_call x2, Pallas kernels, project(): pl.pallas_call(partial(project_kernel, heads), grid_spec=pltpu.PrefetchSc...  19 us
  transfers between devices with their start and end apart: 47, of which 18 were waited for; matrix products, arithmetic and copies ran while one was open for 10% of the time, Pallas kernels for 43%

profile of v2, /device:TPU:0, one launch (start us, length us, event | category | flops | bytes accessed | tf_op | source)
XLA Modules:
  0.0 422.3 jit_solution(7392868362069928801)
XLA Ops:
  9.0 4.1 collective-permute-start.3
  13.1 10.5 %collective-permute-done.3 = bf16[128,896]{1,0:T(8,128)(2,1)S(1)} collective-permute-done((bf16[128,896]{1,0:T(8,128)(2,1)S(1)}, bf16[128,896]{1,0:T(8,128)(2,1)S(1)}, u32[]{:S(2)}, u32[]{:S(2)}) %collective-permute-start.3) | collective-permute-done | bytes 229408 | tf_op jit(solution)/shard_map/ppermute | solution.py:679
  36.4 3.8 fusion.17
  43.8 8.4 %collective-permute-done.6.refs_2_ = bf16[2,128,896]{2,1,0:T(8,128)(2,1)S(1)} collective-permute-done((bf16[2,128,896]{2,1,0:T(8,128)(2,1)S(1)}, bf16[2,128,896]{2,1,0:T(8,128)(2,1)S(1)}, u32[]{:S(2)}, u32[]{:S(2)}) %collective-permute-start.6) | collective-permute-done | bytes 458784 | tf_op jit(solution)/shard_map/ppermute | solution.py:679
  61.0 9.4 %project_0.1 = (f32[4,512,1024]{2,1,0:T(8,128)}, bf16[4,512,512]{2,1,0:T(8,128)(2,1)}, bf16[4,512,512]{2,1,0:T(8,128)(2,1)}, bf16[4,512,512]{2,1,0:T(8,128)(2,1)}) custom-call(s32[4]{0:T(128)} %pad_add_fusion.info_ref.refs_0_, bf16[512,1024]{1,0:T(8,128)(2,1)} %copy-done.7, bf16[512,1024]{1,0:T(8,128)(2,1)} %copy-done.23, ...), custom_call_target="tpu_custom_call" | custom-call | flops 1610612736 | bytes 14155776 | tf_op jit(solution)/shard_map/project_0/pallas_call | solution.py:215
  71.9 3.7 collective-permute-start.10
  75.6 4.2 collective-permute-start.11
  80.8 9.6 %project_1.1 = (f32[4,512,1024]{2,1,0:T(8,128)}, bf16[4,512,512]{2,1,0:T(8,128)(2,1)}, bf16[4,512,512]{2,1,0:T(8,128)(2,1)}, bf16[4,512,512]{2,1,0:T(8,128)(2,1)}) custom-call(s32[4]{0:T(128)} %pad_add_fusion.info_ref.refs_0_, bf16[512,1024]{1,0:T(8,128)(2,1)} %copy-done.6, ...), custom_call_target="tpu_custom_call", output_to_operand_aliasing={{0}: (7, {}), {1}: (8, {}), {2}: (9, {}), {3}: (10, {})} | custom-call | flops 1610612736 | bytes 14155776 | tf_op jit(solution)/shard_map/project_1/pallas_call | solution.py:215
  90.4 4.5 %collective-permute-done.11 = bf16[128,1280]{1,0:T(8,128)(2,1)S(1)} collective-permute-done((bf16[128,1280]{1,0:T(8,128)(2,1)S(1)}, bf16[128,1280]{1,0:T(8,128)(2,1)S(1)}, u32[]{:S(2)}, u32[]{:S(2)}) %collective-permute-start.11) | collective-permute-done | bytes 327712 | tf_op jit(solution)/shard_map/ppermute | solution.py:679
  98.8 12.3 %attention_forward_0.1 = (f32[2048,128]{1,0:T(8,128)}, bf16[2048,256]{1,0:T(8,128)(2,1)}) custom-call(s32[4]{0:T(128)} %pad_add_fusion.info_ref.refs_0_, bf16[2048,512]{1,0:T(8,128)(2,1)} %bitcast.83, bf16[2048,512]{1,0:T(8,128)(2,1)} %bitcast.71, bf16[2048,512]{1,0:T(8,128)(2,1)} %bitcast.77, bf16[2,128,1280]{2,1,0:T(8,128)(2,1)} %copy-done.10), custom_call_target="tpu_custom_call" | custom-call | flops 4294967296 | bytes 2621440 | tf_op jit(solution)/shard_map/attention_forward_0/pallas_call | solution.py:273
  124.2 6.7 %collective-permute-done.17.refs_3_ = bf16[128,1280]{1,0:T(8,128)(2,1)S(1)} collective-permute-done((bf16[128,1280]{1,0:T(8,128)(2,1)S(1)}, bf16[128,1280]{1,0:T(8,128)(2,1)S(1)}, u32[]{:S(2)}, u32[]{:S(2)}) %collective-permute-start.17) | collective-permute-done | bytes 327712 | tf_op jit(solution)/shard_map/ppermute | solution.py:679
  132.5 12.2 %attention_forward_1.1 = (f32[2048,128]{1,0:T(8,128)}, bf16[2048,256]{1,0:T(8,128)(2,1)}) custom-call(s32[4]{0:T(128)} %pad_add_fusion.info_ref.refs_0_, bf16[2048,512]{1,0:T(8,128)(2,1)} %bitcast.84, bf16[2048,512]{1,0:T(8,128)(2,1)} %bitcast.72, bf16[2048,512]{1,0:T(8,128)(2,1)} %bitcast.78, f32[2048,128]{1,0:T(8,128)} %get-tuple-element.166.refs_4_.refs_1_.refs_7_, ...), custom_call_target="tpu_custom_call" | custom-call | flops 4294967296 | bytes 2621440 | tf_op jit(solution)/shard_map/attention_forward_1/pallas_call | solution.py:273
  148.7 3.3 assemble_ffn.2
  160.6 21.6 %feed_forward.1 = (bf16[2,512,1024]{2,1,0:T(8,128)(2,1)}, bf16[2,512,1024]{2,1,0:T(8,128)(2,1)}, bf16[2048,1024]{1,0:T(8,128)(2,1)}, f32[2048,1024]{1,0:T(8,128)}) custom-call(f32[2048,1024]{1,0:T(8,128)} %bitcast.67, f32[2048,128]{1,0:T(8,128)} %get-tuple-element.166.refs_4_.refs_1_.refs_7_, f32[2048,128]{1,0:T(8,128)} %get-tuple-element.172.refs_2_.refs_8_, ...), custom_call_target="tpu_custom_call" | custom-call | flops 8589934592 | bytes 33554432 | tf_op jit(solution)/shard_map/feed_forward/pallas_call | solution.py:341
  182.2 3.3 collective-permute-start.27
  197.3 33.6 %feed_back.1 = (f32[2048,1024]{1,0:T(8,128)}, bf16[2048,256]{1,0:T(8,128)(2,1)}, bf16[2048,256]{1,0:T(8,128)(2,1)}, bf16[1024,2432]{1,0:T(8,128)(2,1)}) custom-call(f32[2048,1024]{1,0:T(8,128)} %bitcast.68, bf16[2048,1024]{1,0:T(8,128)(2,1)} %get-tuple-element.200.refs_1_, f32[2048,1024]{1,0:T(8,128)} %get-tuple-element.201.refs_2_, ...), custom_call_target="tpu_custom_call" | custom-call | flops 17179869184 | bytes 41943040 | tf_op jit(solution)/shard_map/feed_back/pallas_call | solution.py:426
  236.1 16.3 %attention_backward_0a.1 = (bf16[2,512,384]{2,1,0:T(8,128)(2,1)}, f32[2,2,512,128]{3,2,1,0:T(8,128)}, f32[2,2,512,128]{3,2,1,0:T(8,128)}, f32[2,2,512,128]{3,2,1,0:T(8,128)}) custom-call(s32[4]{0:T(128)} %pad_add_fusion.info_ref.refs_0_, bf16[2048,256]{1,0:T(8,128)(2,1)} %get-tuple-element.210.refs_1_, bf16[2048,256]{1,0:T(8,128)(2,1)} %get-tuple-element.211.refs_2_, ...), custom_call_target="tpu_custom_call" | custom-call | flops 4697620480 | bytes 6291456 | tf_op jit(solution)/shard_map/attention_backward_0a/pallas_call | solution.py:556
  252.4 16.7 %attention_backward_1a.1 = (bf16[2,512,384]{2,1,0:T(8,128)(2,1)}, f32[2,2,512,128]{3,2,1,0:T(8,128)}, f32[2,2,512,128]{3,2,1,0:T(8,128)}, f32[2,2,512,128]{3,2,1,0:T(8,128)}) custom-call(s32[4]{0:T(128)} %pad_add_fusion.info_ref.refs_0_, bf16[2048,256]{1,0:T(8,128)(2,1)} %get-tuple-element.222.refs_1_, bf16[2048,256]{1,0:T(8,128)(2,1)} %get-tuple-element.223.refs_2_, ...), custom_call_target="tpu_custom_call" | custom-call | flops 4697620480 | bytes 6291456 | tf_op jit(solution)/shard_map/attention_backward_1a/pallas_call | solution.py:556
  269.1 10.7 %project_back_a.1 = (bf16[2,512,1024]{2,1,0:T(8,128)(2,1)}, f32[1024,768]{1,0:T(8,128)}, f32[8,1024]{1,0:T(8,128)}) custom-call(s32[4]{0:T(128)} %pad_add_fusion.info_ref.refs_0_, bf16[2,512,384]{2,1,0:T(8,128)(2,1)} %get-tuple-element.221.refs_6_.refs_1_, bf16[2,512,384]{2,1,0:T(8,128)(2,1)} %get-tuple-element.224.refs_2_, ...), custom_call_target="tpu_custom_call" | custom-call | flops 3221225472 | bytes 12582912 | tf_op jit(solution)/shard_map/project_back_a/pallas_call | solution.py:615
  279.9 12.0 %collective-permute-start.32 = (bf16[2,512,1024]{2,1,0:T(8,128)(2,1)}, bf16[2,512,1024]{2,1,0:T(8,128)(2,1)S(1)}, u32[]{:S(2)}, u32[]{:S(2)}) collective-permute-start(bf16[2,512,1024]{2,1,0:T(8,128)(2,1)} %get-tuple-element.226), channel_id=1, source_target_pairs={{0,4},{1,5},{6,2},{7,3},{8,12},{9,13},{14,10},{15,11},{16,20},{17,... | collective-permute-start | bytes 6291464 | tf_op jit(solution)/shard_map/ppermute | solution.py:679
  291.9 3.7 collective-permute-done.32
  302.0 9.8 %attention_backward_0b.1.refs_9_.refs_1_ = bf16[2,512,384]{2,1,0:T(8,128)(2,1)} custom-call(s32[4]{0:T(128)} %pad_add_fusion.info_ref.refs_0_, bf16[2048,256]{1,0:T(8,128)(2,1)} %get-tuple-element.210.refs_1_, bf16[2048,256]{1,0:T(8,128)(2,1)} %get-tuple-element.211.refs_2_, bf16[2048,512]{1,0:T(8,128)(2,1)} %bitcast.75, bf16[2048,512]{1,0:T(8,128)(2,1)} %bitcast.81, ...), custom_call_target="tpu_custom_call" | custom-call | flops 2013265920 | bytes 6291456 | tf_op jit(solution)/shard_map/attention_backward_0b/pallas_call | solution.py:556
  314.9 9.8 %attention_backward_1b.1.refs_2_ = bf16[2,512,384]{2,1,0:T(8,128)(2,1)} custom-call(s32[4]{0:T(128)} %pad_add_fusion.info_ref.refs_0_, bf16[2048,256]{1,0:T(8,128)(2,1)} %get-tuple-element.222.refs_1_, bf16[2048,256]{1,0:T(8,128)(2,1)} %get-tuple-element.223.refs_2_, bf16[2048,512]{1,0:T(8,128)(2,1)} %bitcast.76, bf16[2048,512]{1,0:T(8,128)(2,1)} %bitcast.82, ...), custom_call_target="tpu_custom_call" | custom-call | flops 2013265920 | bytes 6291456 | tf_op jit(solution)/shard_map/attention_backward_1b/pallas_call | solution.py:556
  326.9 4.7 %collective-permute-start.34 = (bf16[128,2432]{1,0:T(8,128)(2,1)S(1)}, bf16[128,2432]{1,0:T(8,128)(2,1)S(1)}, u32[]{:S(2)}, u32[]{:S(2)}) collective-permute-start(bf16[128,2432]{1,0:T(8,128)(2,1)S(1)} %get-tuple-element.284), channel_id=1, source_target_pairs={{0,4},{1,5},{2,6},{3,7},{4,0},{5,1},{6,2},{7,3},{8,12},{9,13},{10,... | collective-permute-start | bytes 1867784 | tf_op jit(solution)/shard_map/ppermute | solution.py:679
  335.2 11.1 %project_back_b.1 = (bf16[2,512,1024]{2,1,0:T(8,128)(2,1)}, bf16[2,128,896]{2,1,0:T(8,128)(2,1)}, bf16[2,128,896]{2,1,0:T(8,128)(2,1)}, bf16[2,128,896]{2,1,0:T(8,128)(2,1)}, bf16[2,128,896]{2,1,0:T(8,128)(2,1)}) custom-call(s32[4]{0:T(128)} %pad_add_fusion.info_ref.refs_0_, bf16[2,512,384]{2,1,0:T(8,128)(2,1)} %attention_backward_0b.1.refs_9_.refs_1_, ...), custom_call_target="tpu_custom_call" | custom-call | flops 3221225472 | bytes 12582912 | tf_op jit(solution)/shard_map/project_back_b/pallas_call | solution.py:615
  348.5 13.2 %collective-permute-start.41 = (bf16[128,2432]{1,0:T(8,128)(2,1)S(1)}, bf16[128,2432]{1,0:T(8,128)(2,1)S(1)}, u32[]{:S(2)}, u32[]{:S(2)}) collective-permute-start(bf16[128,2432]{1,0:T(8,128)(2,1)S(1)} %copy-done.11), channel_id=1, source_target_pairs={{0,2},{1,3},{2,0},{3,1},{4,6},{5,7},{6,4},{7,5},{8,10},{9,11},{10,... | collective-permute-start | bytes 1867784 | tf_op jit(solution)/shard_map/ppermute | solution.py:679
  367.9 5.9 %collective-permute-start.37 = (bf16[512,1024]{1,0:T(8,128)(2,1)S(1)}, bf16[512,1024]{1,0:T(8,128)(2,1)S(1)}, u32[]{:S(2)}, u32[]{:S(2)}) collective-permute-start(bf16[512,1024]{1,0:T(8,128)(2,1)S(1)} %fusion.20), channel_id=1, source_target_pairs={{0,1},{1,0},{6,7},{7,6},{8,9},{9,8},{14,15},{15,14},{16,17},{17,16... | collective-permute-start | bytes 3145736 | tf_op jit(solution)/shard_map/ppermute | solution.py:679
  375.0 9.5 %collective-permute-done.39 = bf16[2,128,896]{2,1,0:T(8,128)(2,1)S(1)} collective-permute-done((bf16[2,128,896]{2,1,0:T(8,128)(2,1)S(1)}, bf16[2,128,896]{2,1,0:T(8,128)(2,1)S(1)}, u32[]{:S(2)}, u32[]{:S(2)}) %collective-permute-start.39) | collective-permute-done | bytes 458784 | tf_op jit(solution)/shard_map/ppermute | solution.py:679
  384.6 3.4 collective-permute-done.41
  392.3 6.3 %collective-permute-done.37 = bf16[512,1024]{1,0:T(8,128)(2,1)S(1)} collective-permute-done((bf16[512,1024]{1,0:T(8,128)(2,1)S(1)}, bf16[512,1024]{1,0:T(8,128)(2,1)S(1)}, u32[]{:S(2)}, u32[]{:S(2)}) %collective-permute-start.37) | collective-permute-done | bytes 1048608 | tf_op jit(solution)/shard_map/ppermute | solution.py:679
  398.6 3.5 collective-permute-start.43
  407.3 6.4 %collective-permute-done.43 = bf16[128,896]{1,0:T(8,128)(2,1)S(1)} collective-permute-done((bf16[128,896]{1,0:T(8,128)(2,1)S(1)}, bf16[128,896]{1,0:T(8,128)(2,1)S(1)}, u32[]{:S(2)}, u32[]{:S(2)}) %collective-permute-start.43) | collective-permute-done | bytes 229408 | tf_op jit(solution)/shard_map/ppermute | solution.py:679
  (230 shorter events, 112.9 us)
Async XLA Ops:
  7.2 317.5 %reduce-scatter.2.cloned.1.call-start = ((), (), s32[]{:S(2)}) async-start(), calls=%async_computation.1 | async-start | bytes 6225920 | tf_op jit(solution)/shard_map/reduce_scatter | solution.py:824
  9.0 14.6 %collective-permute-start.3 = (bf16[128,896]{1,0:T(8,128)(2,1)S(1)}, bf16[128,896]{1,0:T(8,128)(2,1)S(1)}, u32[]{:S(2)}, u32[]{:S(2)}) collective-permute-start(bf16[128,896]{1,0:T(8,128)(2,1)S(1)} %fusion.24), channel_id=1, source_target_pairs={{0,2},{1,3},{2,0},{3,1},{4,6},{5,7},{6,4},{7,5},{8,10},{9,11},{10,... | collective-permute-start | bytes 688136 | tf_op jit(solution)/shard_map/ppermute | solution.py:679
  13.1 12.3 %collective-permute-start = (s32[2048]{0:T(1024)}, s32[2048]{0:T(1024)S(1)}, u32[]{:S(2)}, u32[]{:S(2)}) collective-permute-start(s32[2048]{0:T(1024)} %param.17), channel_id=1, source_target_pairs={{0,4},{1,5},{2,6},{3,7},{4,0},{5,1},{6,2},{7,3},{8,12},{9,13},{10,... | collective-permute-start | bytes 24584 | tf_op jit(solution)/shard_map/ppermute | solution.py:679
  25.4 30.4 %collective-permute-start.1 = (bf16[512,1024]{1,0:T(8,128)(2,1)}, bf16[512,1024]{1,0:T(8,128)(2,1)S(1)}, u32[]{:S(2)}, u32[]{:S(2)}) collective-permute-start(bf16[512,1024]{1,0:T(8,128)(2,1)} %param.9), channel_id=1, source_target_pairs={{2,4},{3,5},{4,2},{5,3},{10,12},{11,13},{12,10},{13,11},{18,20},{1... | collective-permute-start | bytes 3145736 | tf_op jit(solution)/shard_map/ppermute | solution.py:679
  26.1 29.7 %collective-permute-start.2 = (bf16[512,1024]{1,0:T(8,128)(2,1)}, bf16[512,1024]{1,0:T(8,128)(2,1)S(1)}, u32[]{:S(2)}, u32[]{:S(2)}) collective-permute-start(bf16[512,1024]{1,0:T(8,128)(2,1)} %param.9), channel_id=1, source_target_pairs={{0,1},{1,0},{6,7},{7,6},{8,9},{9,8},{14,15},{15,14},{16,17},{17,16... | collective-permute-start | bytes 3145736 | tf_op jit(solution)/shard_map/ppermute | solution.py:679
  28.9 15.0 %collective-permute-start.5 = (bf16[2,128,896]{2,1,0:T(8,128)(2,1)S(1)}, bf16[2,128,896]{2,1,0:T(8,128)(2,1)S(1)}, u32[]{:S(2)}, u32[]{:S(2)}) collective-permute-start(bf16[2,128,896]{2,1,0:T(8,128)(2,1)S(1)} %pad_maximum_fusion.6.refs_0_), channel_id=1, source_target_pairs={{0,8},{1,9},{2,10},{3,11},{4,12},{5,13},{6,14},{7,15},{8,0},{9,1},... | collective-permute-start | bytes 1376264 | tf_op jit(solution)/shard_map/ppermute | solution.py:679
  30.4 21.8 %collective-permute-start.6 = (bf16[2,128,896]{2,1,0:T(8,128)(2,1)S(1)}, bf16[2,128,896]{2,1,0:T(8,128)(2,1)S(1)}, u32[]{:S(2)}, u32[]{:S(2)}) collective-permute-start(bf16[2,128,896]{2,1,0:T(8,128)(2,1)S(1)} %pad_maximum_fusion.6.refs_0_), channel_id=1, source_target_pairs={{0,16},{1,17},{2,18},{3,19},{4,20},{5,21},{6,22},{7,23},{8,24},{9,... | collective-permute-start | bytes 1376264 | tf_op jit(solution)/shard_map/ppermute | solution.py:679
  31.9 21.0 %collective-permute-start.7 = (bf16[2,128,896]{2,1,0:T(8,128)(2,1)S(1)}, bf16[2,128,896]{2,1,0:T(8,128)(2,1)}, u32[]{:S(2)}, u32[]{:S(2)}) collective-permute-start(bf16[2,128,896]{2,1,0:T(8,128)(2,1)S(1)} %pad_maximum_fusion.6.refs_0_), channel_id=1, source_target_pairs={{0,24},{1,25},{2,26},{3,27},{4,28},{5,29},{6,30},{7,31},{8,16},{9,... | collective-permute-start | bytes 1376264 | tf_op jit(solution)/shard_map/ppermute | solution.py:679
  57.4 13.1 %collective-permute-start.9 = (bf16[512,1024]{1,0:T(8,128)(2,1)}, bf16[512,1024]{1,0:T(8,128)(2,1)}, u32[]{:S(2)}, u32[]{:S(2)}) collective-permute-start(bf16[512,1024]{1,0:T(8,128)(2,1)} %copy-done.25), channel_id=1, source_target_pairs={{2,3},{3,2},{4,5},{5,4},{10,11},{11,10},{12,13},{13,12},{18,19},{1... | collective-permute-start | bytes 3145736 | tf_op jit(solution)/shard_map/ppermute | solution.py:679
  75.6 19.2 %collective-permute-start.11 = (bf16[128,1280]{1,0:T(8,128)(2,1)S(1)}, bf16[128,1280]{1,0:T(8,128)(2,1)S(1)}, u32[]{:S(2)}, u32[]{:S(2)}) collective-permute-start(bf16[128,1280]{1,0:T(8,128)(2,1)S(1)} %constant_dynamic-update-slice_fusion), channel_id=1, source_target_pairs={{0,2},{1,3},{2,0},{3,1},{4,6},{5,7},{6,4},{7,5},{8,10},{9,11},{10,... | collective-permute-start | bytes 983048 | tf_op jit(solution)/shard_map/ppermute | solution.py:679
  96.7 16.8 %collective-permute-start.13 = (bf16[2,128,1280]{2,1,0:T(8,128)(2,1)S(1)}, bf16[2,128,1280]{2,1,0:T(8,128)(2,1)S(1)}, u32[]{:S(2)}, u32[]{:S(2)}) collective-permute-start(bf16[2,128,1280]{2,1,0:T(8,128)(2,1)S(1)} %pad_maximum_fusion.4.refs_4_.refs_0_), channel_id=1, source_target_pairs={{0,8},{1,9},{2,10},{3,11},{4,12},{5,13},{6,14},{7,15},{8,0},{9,1},... | collective-permute-start | bytes 1966088 | tf_op jit(solution)/shard_map/ppermute | solution.py:679
  97.1 16.6 %collective-permute-start.14 = (bf16[2,128,1280]{2,1,0:T(8,128)(2,1)S(1)}, bf16[2,128,1280]{2,1,0:T(8,128)(2,1)}, u32[]{:S(2)}, u32[]{:S(2)}) collective-permute-start(bf16[2,128,1280]{2,1,0:T(8,128)(2,1)S(1)} %pad_maximum_fusion.4.refs_4_.refs_0_), channel_id=1, source_target_pairs={{0,16},{1,17},{2,18},{3,19},{4,20},{5,21},{6,22},{7,23},{8,24},{9,... | collective-permute-start | bytes 1966088 | tf_op jit(solution)/shard_map/ppermute | solution.py:679
  98.8 14.5 %collective-permute-start.15 = (bf16[128,1024]{1,0:T(8,128)(2,1)}, bf16[128,1024]{1,0:T(8,128)(2,1)S(1)}, u32[]{:S(2)}, u32[]{:S(2)}) collective-permute-start(bf16[128,1024]{1,0:T(8,128)(2,1)} %param.13), channel_id=1, source_target_pairs={{0,2},{1,3},{2,0},{3,1},{4,6},{5,7},{6,4},{7,5},{8,10},{9,11},{10,... | collective-permute-start | bytes 786440 | tf_op jit(solution)/shard_map/ppermute | solution.py:679
  114.7 43.6 %collective-permute-start.23 = (bf16[512,1024]{1,0:T(8,128)(2,1)S(1)}, bf16[512,1024]{1,0:T(8,128)(2,1)}, u32[]{:S(2)}, u32[]{:S(2)}) collective-permute-start(bf16[512,1024]{1,0:T(8,128)(2,1)S(1)} %copy-done.5), channel_id=1, source_target_pairs={{2,4},{3,5},{4,2},{5,3},{10,12},{11,13},{12,10},{13,11},{18,20},{1... | collective-permute-start | bytes 3145736 | tf_op jit(solution)/shard_map/ppermute | solution.py:679
  116.4 42.0 %collective-permute-start.24 = (bf16[512,1024]{1,0:T(8,128)(2,1)S(1)}, bf16[512,1024]{1,0:T(8,128)(2,1)}, u32[]{:S(2)}, u32[]{:S(2)}) collective-permute-start(bf16[512,1024]{1,0:T(8,128)(2,1)S(1)} %copy-done.5), channel_id=1, source_target_pairs={{0,1},{1,0},{6,7},{7,6},{8,9},{9,8},{14,15},{15,14},{16,17},{17,16... | collective-permute-start | bytes 3145736 | tf_op jit(solution)/shard_map/ppermute | solution.py:679
  122.0 22.8 %collective-permute-start.19 = (bf16[2,128,1024]{2,1,0:T(8,128)(2,1)S(1)}, bf16[2,128,1024]{2,1,0:T(8,128)(2,1)S(1)}, u32[]{:S(2)}, u32[]{:S(2)}) collective-permute-start(bf16[2,128,1024]{2,1,0:T(8,128)(2,1)S(1)} %pad_maximum_fusion.5.refs_5_.refs_0_), channel_id=1, source_target_pairs={{0,8},{1,9},{2,10},{3,11},{4,12},{5,13},{6,14},{7,15},{8,0},{9,1},... | collective-permute-start | bytes 1572872 | tf_op jit(solution)/shard_map/ppermute | solution.py:679
  122.6 22.2 %collective-permute-start.20 = (bf16[2,128,1024]{2,1,0:T(8,128)(2,1)S(1)}, bf16[2,128,1024]{2,1,0:T(8,128)(2,1)}, u32[]{:S(2)}, u32[]{:S(2)}) collective-permute-start(bf16[2,128,1024]{2,1,0:T(8,128)(2,1)S(1)} %pad_maximum_fusion.5.refs_5_.refs_0_), channel_id=1, source_target_pairs={{0,16},{1,17},{2,18},{3,19},{4,20},{5,21},{6,22},{7,23},{8,24},{9,... | collective-permute-start | bytes 1572872 | tf_op jit(solution)/shard_map/ppermute | solution.py:679
  131.7 13.1 %collective-permute-start.18 = (bf16[128,1280]{1,0:T(8,128)(2,1)}, bf16[128,1280]{1,0:T(8,128)(2,1)}, u32[]{:S(2)}, u32[]{:S(2)}) collective-permute-start(bf16[128,1280]{1,0:T(8,128)(2,1)} %slice_bitcast_fusion.5), channel_id=1, source_target_pairs={{0,16},{1,17},{2,18},{3,19},{4,20},{5,21},{6,22},{7,23},{8,24},{9,... | collective-permute-start | bytes 983048 | tf_op jit(solution)/shard_map/ppermute | solution.py:679
  158.5 23.7 %collective-permute-start.26 = (bf16[512,1024]{1,0:T(8,128)(2,1)S(1)}, bf16[512,1024]{1,0:T(8,128)(2,1)}, u32[]{:S(2)}, u32[]{:S(2)}) collective-permute-start(bf16[512,1024]{1,0:T(8,128)(2,1)S(1)} %broadcast_select_fusion.1.refs_7_.refs_3_), channel_id=1, source_target_pairs={{0,4},{1,5},{2,6},{3,7},{4,0},{5,1},{6,2},{7,3},{8,12},{9,13},{10,... | collective-permute-start | bytes 3145736 | tf_op jit(solution)/shard_map/ppermute | solution.py:679
  158.6 23.7 %collective-permute-start.25 = (bf16[512,1024]{1,0:T(8,128)(2,1)}, bf16[512,1024]{1,0:T(8,128)(2,1)}, u32[]{:S(2)}, u32[]{:S(2)}) collective-permute-start(bf16[512,1024]{1,0:T(8,128)(2,1)} %collective-permute-done.23), channel_id=1, source_target_pairs={{2,3},{3,2},{4,5},{5,4},{10,11},{11,10},{12,13},{13,12},{18,19},{1... | collective-permute-start | bytes 3145736 | tf_op jit(solution)/shard_map/ppermute | solution.py:679
  193.5 37.4 %collective-permute-start.29 = (bf16[512,1024]{1,0:T(8,128)(2,1)}, bf16[512,1024]{1,0:T(8,128)(2,1)}, u32[]{:S(2)}, u32[]{:S(2)}) collective-permute-start(bf16[512,1024]{1,0:T(8,128)(2,1)} %fusion.18.refs_13_), channel_id=1, source_target_pairs={{2,3},{3,2},{4,5},{5,4},{10,11},{11,10},{12,13},{13,12},{18,19},{1... | collective-permute-start | bytes 3145736 | tf_op jit(solution)/shard_map/ppermute | solution.py:679
  195.1 35.8 %collective-permute-start.30 = (bf16[512,1024]{1,0:T(8,128)(2,1)}, bf16[512,1024]{1,0:T(8,128)(2,1)S(1)}, u32[]{:S(2)}, u32[]{:S(2)}) collective-permute-start(bf16[512,1024]{1,0:T(8,128)(2,1)} %fusion.18.refs_13_), channel_id=1, source_target_pairs={{0,1},{1,0},{6,7},{7,6},{8,9},{9,8},{14,15},{15,14},{16,17},{17,16... | collective-permute-start | bytes 3145736 | tf_op jit(solution)/shard_map/ppermute | solution.py:679
  235.2 17.2 %collective-permute-start.31 = (bf16[512,1024]{1,0:T(8,128)(2,1)}, bf16[512,1024]{1,0:T(8,128)(2,1)S(1)}, u32[]{:S(2)}, u32[]{:S(2)}) collective-permute-start(bf16[512,1024]{1,0:T(8,128)(2,1)} %add_convert_fusion.refs_6_), channel_id=1, source_target_pairs={{2,4},{3,5},{4,2},{5,3},{10,12},{11,13},{12,10},{13,11},{18,20},{1... | collective-permute-start | bytes 3145736 | tf_op jit(solution)/shard_map/ppermute | solution.py:679
  279.9 15.7 %collective-permute-start.32 = (bf16[2,512,1024]{2,1,0:T(8,128)(2,1)}, bf16[2,512,1024]{2,1,0:T(8,128)(2,1)S(1)}, u32[]{:S(2)}, u32[]{:S(2)}) collective-permute-start(bf16[2,512,1024]{2,1,0:T(8,128)(2,1)} %get-tuple-element.226), channel_id=1, source_target_pairs={{0,4},{1,5},{6,2},{7,3},{8,12},{9,13},{14,10},{15,11},{16,20},{17,... | collective-permute-start | bytes 6291464 | tf_op jit(solution)/shard_map/ppermute | solution.py:679
  331.6 14.8 %collective-permute-start.35 = (bf16[512,1024]{1,0:T(8,128)(2,1)S(1)}, bf16[512,1024]{1,0:T(8,128)(2,1)}, u32[]{:S(2)}, u32[]{:S(2)}) collective-permute-start(bf16[512,1024]{1,0:T(8,128)(2,1)S(1)} %copy-done.9), channel_id=1, source_target_pairs={{2,4},{3,5},{4,2},{5,3},{10,12},{11,13},{12,10},{13,11},{18,20},{1... | collective-permute-start | bytes 3145736 | tf_op jit(solution)/shard_map/ppermute | solution.py:679
  346.4 18.8 %collective-permute-start.36 = (bf16[2,512,1024]{2,1,0:T(8,128)(2,1)}, bf16[2,512,1024]{2,1,0:T(8,128)(2,1)S(1)}, u32[]{:S(2)}, u32[]{:S(2)}) collective-permute-start(bf16[2,512,1024]{2,1,0:T(8,128)(2,1)} %get-tuple-element.242), channel_id=1, source_target_pairs={{2,6},{3,7},{4,0},{5,1},{10,14},{11,15},{12,8},{13,9},{18,22},{19,... | collective-permute-start | bytes 6291464 | tf_op jit(solution)/shard_map/ppermute | solution.py:679
  348.5 39.5 %collective-permute-start.41 = (bf16[128,2432]{1,0:T(8,128)(2,1)S(1)}, bf16[128,2432]{1,0:T(8,128)(2,1)S(1)}, u32[]{:S(2)}, u32[]{:S(2)}) collective-permute-start(bf16[128,2432]{1,0:T(8,128)(2,1)S(1)} %copy-done.11), channel_id=1, source_target_pairs={{0,2},{1,3},{2,0},{3,1},{4,6},{5,7},{6,4},{7,5},{8,10},{9,11},{10,... | collective-permute-start | bytes 1867784 | tf_op jit(solution)/shard_map/ppermute | solution.py:679
  361.7 13.3 %collective-permute-start.38 = (bf16[2,128,896]{2,1,0:T(8,128)(2,1)S(1)}, bf16[2,128,896]{2,1,0:T(8,128)(2,1)S(1)}, u32[]{:S(2)}, u32[]{:S(2)}) collective-permute-start(bf16[2,128,896]{2,1,0:T(8,128)(2,1)S(1)} %copy-done.39), channel_id=1, source_target_pairs={{0,8},{1,9},{2,10},{3,11},{4,12},{5,13},{6,14},{7,15},{8,0},{9,1},... | collective-permute-start | bytes 1376264 | tf_op jit(solution)/shard_map/ppermute | solution.py:679
  362.1 22.4 %collective-permute-start.39 = (bf16[2,128,896]{2,1,0:T(8,128)(2,1)S(1)}, bf16[2,128,896]{2,1,0:T(8,128)(2,1)S(1)}, u32[]{:S(2)}, u32[]{:S(2)}) collective-permute-start(bf16[2,128,896]{2,1,0:T(8,128)(2,1)S(1)} %copy-done.38), channel_id=1, source_target_pairs={{0,16},{1,17},{2,18},{3,19},{4,20},{5,21},{6,22},{7,23},{8,24},{9,... | collective-permute-start | bytes 1376264 | tf_op jit(solution)/shard_map/ppermute | solution.py:679
  362.8 21.8 %collective-permute-start.40 = (bf16[2,128,896]{2,1,0:T(8,128)(2,1)S(1)}, bf16[2,128,896]{2,1,0:T(8,128)(2,1)S(1)}, u32[]{:S(2)}, u32[]{:S(2)}) collective-permute-start(bf16[2,128,896]{2,1,0:T(8,128)(2,1)S(1)} %copy-done.37), channel_id=1, source_target_pairs={{0,24},{1,25},{2,26},{3,27},{4,28},{5,29},{6,30},{7,31},{8,16},{9,... | collective-permute-start | bytes 1376264 | tf_op jit(solution)/shard_map/ppermute | solution.py:679
  367.9 30.7 %collective-permute-start.37 = (bf16[512,1024]{1,0:T(8,128)(2,1)S(1)}, bf16[512,1024]{1,0:T(8,128)(2,1)S(1)}, u32[]{:S(2)}, u32[]{:S(2)}) collective-permute-start(bf16[512,1024]{1,0:T(8,128)(2,1)S(1)} %fusion.20), channel_id=1, source_target_pairs={{0,1},{1,0},{6,7},{7,6},{8,9},{9,8},{14,15},{15,14},{16,17},{17,16... | collective-permute-start | bytes 3145736 | tf_op jit(solution)/shard_map/ppermute | solution.py:679
  398.6 15.1 %collective-permute-start.43 = (bf16[128,896]{1,0:T(8,128)(2,1)S(1)}, bf16[128,896]{1,0:T(8,128)(2,1)S(1)}, u32[]{:S(2)}, u32[]{:S(2)}) collective-permute-start(bf16[128,896]{1,0:T(8,128)(2,1)S(1)} %pad_maximum_fusion.7), channel_id=1, source_target_pairs={{0,2},{1,3},{2,0},{3,1},{4,6},{5,7},{6,4},{7,5},{8,10},{9,11},{10,... | collective-permute-start | bytes 688136 | tf_op jit(solution)/shard_map/ppermute | solution.py:679
  (56 other events, 431.8 us)
Sparse Core Ops, SparseCore 0:
  231.1 57.5 reduce-scatter.1
